TPU v7x, 256 devices: a whole 4x4x8 slice. The times are simulated.
256 devices in a mesh: stream: 2 (over core), depth: 4 (over z_lo), height: 32 (over z_hi, x, y).
Axes of the slice: x: 4, y: 4, z: 8 (z_hi: 2, z_lo: 4; z = z_hi * 4 + z_lo), core: 2. Of those that a mesh axis runs over, the one named last changes fastest.
Arguments:
- tokens: bfloat16 [2, 40, 320, 1920], P('stream', 'depth', 'height'), may hold values from -40 to 40
- ln_gain: float32 [192], replicated, may hold values from 0.1 to 1.9
- w_query: bfloat16 [192, 192], replicated, may hold values from -0.4375 to 0.4375
- w_keyval: bfloat16 [192, 384], replicated, may hold values from -0.4375 to 0.4375
- w_out: bfloat16 [192, 192], replicated, may hold values from -0.4375 to 0.4375
- w_merge: bfloat16 [1536, 384], replicated, may hold values from -0.15625 to 0.15625
- owner_map: int32 [4, 32], P('depth', 'height'), may hold values from 0 to 31, as said below
- relay_grad: bfloat16 [2, 384, 48000], P('stream', ('depth', 'height')), may hold values from -6 to 6
Outputs:
- relayed: bfloat16 [2, 384, 48000], P('stream', ('depth', 'height'))
- token_grad: bfloat16 [2, 40, 320, 1920], P('stream', 'depth', 'height')
- gain_grad: float32 [192], replicated
- query_wgrad: float32 [192, 192], replicated
- keyval_wgrad: float32 [192, 384], replicated
- out_wgrad: float32 [192, 192], replicated
- merge_wgrad: float32 [1536, 384], replicated
Inputs may be any that keep to these rules, and one draw needn't show every extreme that they name: `owner_map`: entry j of row r names the height index of the owner of next-section window j of depth row r: with h = j // 1 the height index that formed it, the owner is h - 1, h or h + 1, taken modulo 32. Every owner receives at most 3 windows, and in every depth row some owner receives exactly 3, all 1 windows of each of its two neighbours among them.
All inputs are finite; a program needn't handle non-finite values.
Results may differ from a plain program's by a relative error of at most 0.0081.
The roundings to bfloat16 on the way count: a program that leaves them out, or rounds other values in their place, can miss the bound.
Values may be sent and summed in bfloat16 or wider, within the bound.
A program may use at most 128 MiB of HBM per device.

v0:
```python
import math

import jax
import jax.numpy as jnp
from jax import lax
from jax.sharding import PartitionSpec as P

C = 192
HEADS = 6
HEAD_DIM = 32


norm_epsilon = 1e-05


def shifted_2(value, axis, by):
    devices = lax.axis_size(axis)
    pairs = [(i, i + by) for i in range(devices) if 0 <= i + by < devices]
    return lax.ppermute(value, axis, pairs)


def shortened(value):
    return jax.tree.map(lambda a: a.astype(jnp.bfloat16) if a.dtype == jnp.float32 else a, value)


def from_partner(value, axis, bit):
    return lax.ppermute(value, axis, [(i, i ^ 1 << bit) for i in range(lax.axis_size(axis))])


def padded(block, sides, width):
    for axis, dim in sides:
        count = lax.axis_size(axis)
        forward = [(i, i + 1) for i in range(count - 1)]
        backward = [(target, source) for source, target in forward]
        low = lax.ppermute(
            lax.slice_in_dim(block, block.shape[dim] - width, None, axis=dim), axis, forward
        )
        high = lax.ppermute(lax.slice_in_dim(block, 0, width, axis=dim), axis, backward)
        block = jnp.concatenate([low, block, high], axis=dim)
    return block


def passed_along(block, axis, distance):
    devices = range(lax.axis_size(axis))
    route = [((i - distance) % len(devices), i) for i in devices]
    return lax.ppermute(block, axis, route)


def normalize(values):
    centre = jnp.mean(values, -1, keepdims=True)
    shifted = values - centre
    inverse = lax.rsqrt(jnp.mean(shifted * shifted, -1, keepdims=True) + norm_epsilon)
    return shifted * inverse


def normalize_back(values, upstream):
    centre = jnp.mean(values, -1, keepdims=True)
    shifted = values - centre
    inverse = lax.rsqrt(jnp.mean(shifted * shifted, -1, keepdims=True) + norm_epsilon)
    normed = shifted * inverse
    return inverse * (
        upstream
        - jnp.mean(upstream, -1, keepdims=True)
        - normed * jnp.mean(upstream * normed, -1, keepdims=True)
    )


def window_rims(tensor, axis_pos, number):
    leading = jnp.moveaxis(tensor, axis_pos, 0)
    middle = leading[1 : number * 5 + 1].reshape((number, 5) + leading.shape[1:])
    before = leading[0 : number * 5 : 5][:, None]
    after_rim = leading[6 : number * 5 + 2 : 5][:, None]
    joined = jnp.concatenate([before, middle, after_rim], 1)
    return jnp.moveaxis(joined, (0, 1), (axis_pos, axis_pos + 1))


def gather_search(region, depth_count, height_count, width_count):
    feature = region.shape[-1]
    search = window_rims(region, 0, depth_count)
    search = window_rims(search, 2, height_count)
    search = window_rims(search, 4, width_count)
    search = jnp.transpose(search, (0, 2, 4, 1, 3, 5, 6))
    return search.reshape(depth_count * height_count * width_count, 343, feature)


def base_windows(volume):
    depth_count, height_count, width_count = (
        volume.shape[0] // 5,
        volume.shape[1] // 5,
        volume.shape[2] // 5,
    )
    feature = volume.shape[3]
    pieces = volume.reshape(depth_count, 5, height_count, 5, width_count, 5, feature)
    pieces = jnp.transpose(pieces, (0, 2, 4, 1, 3, 5, 6))
    return pieces.reshape(depth_count * height_count * width_count, 125, feature)


def window_grid(windows, depth_count, height_count, width_count):
    feature = windows.shape[-1]
    pieces = windows.reshape(depth_count, height_count, width_count, 5, 5, 5, feature)
    pieces = jnp.transpose(pieces, (0, 3, 1, 4, 2, 5, 6))
    return pieces.reshape(depth_count * 5, height_count * 5, width_count * 5, feature)


def to_eight(volume):
    depth_len, height, width_len, feature = volume.shape
    pieces = volume.reshape(depth_len // 2, 2, height // 2, 2, width_len // 2, 2, feature)
    return jnp.transpose(pieces, (0, 2, 4, 1, 3, 5, 6)).reshape(
        depth_len // 2, height // 2, width_len // 2, 8 * feature
    )


def from_eight(volume, feature):
    depth_half, height_half, width_half = volume.shape[:3]
    pieces = volume.reshape(depth_half, height_half, width_half, 2, 2, 2, feature)
    return jnp.transpose(pieces, (0, 3, 1, 4, 2, 5, 6)).reshape(
        2 * depth_half, 2 * height_half, 2 * width_half, feature
    )


def next_windows(volume):
    depth_half, height_half, width_half, feature = volume.shape
    pieces = volume.reshape(depth_half // 5, 5, height_half // 5, 5, width_half // 5, 5, feature)
    return jnp.transpose(pieces, (0, 2, 4, 1, 3, 5, 6)).reshape(
        depth_half // 5, height_half // 5, width_half // 5, 125 * feature
    )


def next_grid(windows, feature):
    depth_blocks, height_blocks, width_blocks = windows.shape[:3]
    pieces = windows.reshape(depth_blocks, height_blocks, width_blocks, 5, 5, 5, feature)
    return jnp.transpose(pieces, (0, 3, 1, 4, 2, 5, 6)).reshape(
        5 * depth_blocks, 5 * height_blocks, 5 * width_blocks, feature
    )


def in_blocks(function, arrays, block_size):
    window_total = arrays[0].shape[0]
    grouped = tuple(
        (
            member.reshape((window_total // block_size, block_size) + member.shape[1:])
            for member in arrays
        )
    )
    result = lax.map(lambda pieces: function(*pieces), grouped)
    return jax.tree.map(
        lambda stacked: stacked.reshape((window_total,) + stacked.shape[2:]), result
    )


def attend_forward(query_w, keyval_w, inside_keys):
    windows = query_w.shape[0]
    query_heads = query_w.reshape(windows, 125, HEADS, HEAD_DIM)
    key_heads = keyval_w[:, :, :C].reshape(windows, 343, HEADS, HEAD_DIM)
    value_heads = keyval_w[:, :, C:].reshape(windows, 343, HEADS, HEAD_DIM)
    scores = jnp.einsum(
        "nqhd,nkhd->nhqk", query_heads, key_heads, preferred_element_type=jnp.float32
    ) * HEAD_DIM ** (-0.5)
    weights = jnp.exp(scores) * inside_keys[:, None, None, :]
    attention_b = (weights / jnp.sum(weights, -1, keepdims=True)).astype(jnp.bfloat16)
    context = jnp.einsum(
        "nhqk,nkhd->nqhd", attention_b, value_heads, preferred_element_type=jnp.float32
    )
    return (context.reshape(query_w.shape).astype(jnp.bfloat16), attention_b)


def attend_backward(query_w, keyval_w, attention_b, context_grad):
    windows = query_w.shape[0]
    query_heads = query_w.reshape(windows, 125, HEADS, HEAD_DIM)
    key_heads = keyval_w[:, :, :C].reshape(windows, 343, HEADS, HEAD_DIM)
    value_heads = keyval_w[:, :, C:].reshape(windows, 343, HEADS, HEAD_DIM)
    grad_heads = context_grad.reshape(windows, 125, HEADS, HEAD_DIM)
    weight_grad = jnp.einsum(
        "nqhd,nkhd->nhqk", grad_heads, value_heads, preferred_element_type=jnp.float32
    )
    value_grad = jnp.einsum(
        "nhqk,nqhd->nkhd", attention_b, grad_heads, preferred_element_type=jnp.float32
    )
    attention = attention_b.astype(jnp.float32)
    score_grad = (
        attention
        * (weight_grad - jnp.sum(weight_grad * attention, -1, keepdims=True))
        * HEAD_DIM ** (-0.5)
    ).astype(jnp.bfloat16)
    query_grad = jnp.einsum(
        "nhqk,nkhd->nqhd", score_grad, key_heads, preferred_element_type=jnp.float32
    )
    key_grad = jnp.einsum(
        "nhqk,nqhd->nkhd", score_grad, query_heads, preferred_element_type=jnp.float32
    )
    return (
        query_grad.reshape(windows, 125, C),
        jnp.concatenate([key_grad, value_grad], 2).reshape(windows, 343, 2 * C),
    )


def fold_rims(extended):
    from_next = shifted_2(extended[:, :1].astype(jnp.bfloat16), "height", -1).astype(jnp.float32)
    from_prior = shifted_2(extended[:, -1:].astype(jnp.bfloat16), "height", 1).astype(jnp.float32)
    middle = extended[:, 1:-1]
    middle = jnp.concatenate(
        [middle[:, :1] + from_prior, middle[:, 1:-1], middle[:, -1:] + from_next], 1
    )
    depth_next = shifted_2(shortened(middle[:1]), "depth", -1)
    depth_prior = shifted_2(shortened(middle[-1:]), "depth", 1)
    interior = middle[1:-1]
    return jnp.concatenate(
        [interior[:1] + depth_prior, interior[1:-1], interior[-1:] + depth_next], 0
    )


def local(tokens, ln_gain, w_query, w_keyval, w_out, w_merge, owner_map, relay_grad):
    depth_len, height_len = (tokens.shape[1], tokens.shape[2])
    width_len = tokens.shape[3] // C
    depth_count, height_count, width_count = (depth_len // 5, height_len // 5, width_len // 5)
    block_size = math.gcd(depth_count * height_count * width_count, 8)
    values = tokens.reshape(depth_len, height_len, width_len, C).astype(jnp.float32)
    normed = normalize(values)
    normal_rows = (normed * ln_gain).astype(jnp.bfloat16).reshape(-1, C)
    query_rows = jnp.dot(normal_rows, w_query, preferred_element_type=jnp.float32).astype(
        jnp.bfloat16
    )
    keyval_rows = jnp.dot(normal_rows, w_keyval, preferred_element_type=jnp.float32).astype(
        jnp.bfloat16
    )
    swapped = from_partner(
        keyval_rows.reshape(depth_len, height_len, width_len * 2 * C), "stream", 0
    )
    rimmed = padded(swapped, (("depth", 0), ("height", 1)), 1)
    partner_keyval = rimmed.reshape(depth_len + 2, height_len + 2, width_len, 2 * C)
    partner_keyval = jnp.pad(partner_keyval, ((0, 0), (0, 0), (1, 1), (0, 0)))
    depth_place = (
        lax.axis_index("depth") * depth_len - 1 + jnp.arange(depth_len + 2, dtype=jnp.int32)
    )
    height_place = (
        lax.axis_index("height") * height_len - 1 + jnp.arange(height_len + 2, dtype=jnp.int32)
    )
    width_place = jnp.arange(width_len + 2, dtype=jnp.int32)
    depth_inside = ((depth_place >= 0) & (depth_place < depth_len * lax.axis_size("depth"))).astype(
        jnp.float32
    )
    height_inside = (
        (height_place >= 0) & (height_place < height_len * lax.axis_size("height"))
    ).astype(jnp.float32)
    width_inside = ((width_place >= 1) & (width_place <= width_len)).astype(jnp.float32)
    inside = (
        depth_inside[:, None, None, None]
        * height_inside[None, :, None, None]
        * width_inside[None, None, :, None]
    )
    inside_keys = gather_search(inside, depth_count, height_count, width_count)[:, :, 0]
    query_w = base_windows(query_rows.reshape(depth_len, height_len, width_len, C))
    keyval_w = gather_search(partner_keyval, depth_count, height_count, width_count)
    context_w, attention_w = in_blocks(attend_forward, (query_w, keyval_w, inside_keys), block_size)
    context_rows = window_grid(context_w, depth_count, height_count, width_count).reshape(-1, C)
    output = (
        jnp.dot(context_rows, w_out, preferred_element_type=jnp.float32) + values.reshape(-1, C)
    ).astype(jnp.bfloat16)
    eight_cells = to_eight(output.reshape(depth_len, height_len, width_len, C)).reshape(-1, 8 * C)
    merged = jnp.dot(eight_cells, w_merge, preferred_element_type=jnp.float32).astype(jnp.bfloat16)
    next_rows = next_windows(
        merged.reshape(depth_len // 2, height_len // 2, width_len // 2, 2 * C)
    ).reshape(-1, 250 * C)
    targets = owner_map[0]
    win_count = targets.shape[0]
    peer_count = lax.axis_size("height")
    own_index = lax.axis_index("height")
    capacity = 3 * win_count
    window_order = jnp.arange(win_count, dtype=jnp.int32)
    direction = (targets - own_index + 1 + peer_count) % peer_count
    earlier = jnp.sum(
        (
            (targets[None, :] == targets[:, None]) & (window_order[None, :] < window_order[:, None])
        ).astype(jnp.int32),
        1,
    )
    send_slot = direction * win_count + earlier
    send_pick = jnp.arange(3 * win_count, dtype=jnp.int32)[:, None] == send_slot[None, :]
    send_matrix = send_pick.astype(jnp.bfloat16)
    outgoing = (
        jnp.dot(send_matrix, next_rows, preferred_element_type=jnp.float32)
        .astype(jnp.bfloat16)
        .reshape(3, win_count, -1)
    )
    filled = jnp.sum(send_pick.astype(jnp.int32), 1).reshape(3, win_count)
    left_payload, left_flags = passed_along((outgoing[2], filled[2]), "height", 1)
    right_payload, right_flags = passed_along((outgoing[0], filled[0]), "height", -1)
    incoming = jnp.concatenate([left_payload, outgoing[1], right_payload], 0)
    live_slot = jnp.concatenate([left_flags, filled[1], right_flags], 0)
    sources = (own_index + jnp.arange(3, dtype=jnp.int32) - 1 + peer_count) % peer_count
    slot_key = (
        sources[:, None] * win_count + jnp.arange(win_count, dtype=jnp.int32)[None, :]
    ).reshape(-1)
    live_flag = live_slot > 0
    arrival_rank = jnp.sum(
        (live_flag[None, :] & (slot_key[None, :] < slot_key[:, None])).astype(jnp.int32), 1
    )
    take_pick = (
        (arrival_rank[None, :] == jnp.arange(capacity, dtype=jnp.int32)[:, None])
        & live_flag[None, :]
    ).astype(jnp.bfloat16)
    relayed = jnp.dot(take_pick, incoming, preferred_element_type=jnp.float32).astype(jnp.bfloat16)
    backward_slots = (
        jnp.dot(take_pick.T, relay_grad[0], preferred_element_type=jnp.float32)
        .astype(jnp.bfloat16)
        .reshape(3, win_count, -1)
    )
    returned_right = passed_along(backward_slots[0], "height", -1)
    returned_left = passed_along(backward_slots[2], "height", 1)
    returned = jnp.concatenate([returned_left, backward_slots[1], returned_right], 0)
    window_grad = jnp.dot(send_matrix.T, returned, preferred_element_type=jnp.float32).astype(
        jnp.bfloat16
    )
    merged_grad = next_grid(
        window_grad.reshape(depth_len // 10, height_len // 10, width_len // 10, -1), 2 * C
    ).reshape(-1, 2 * C)
    merge_wgrad = jnp.dot(eight_cells.T, merged_grad, preferred_element_type=jnp.float32)
    eight_grad = jnp.dot(merged_grad, w_merge.T, preferred_element_type=jnp.float32).astype(
        jnp.bfloat16
    )
    output_grad = from_eight(
        eight_grad.reshape(depth_len // 2, height_len // 2, width_len // 2, 8 * C), C
    ).reshape(-1, C)
    out_wgrad = jnp.dot(context_rows.T, output_grad, preferred_element_type=jnp.float32)
    context_grad = jnp.dot(output_grad, w_out.T, preferred_element_type=jnp.float32).astype(
        jnp.bfloat16
    )
    context_grad_w = base_windows(context_grad.reshape(depth_len, height_len, width_len, C))
    query_grad_w, keyval_grad_w = in_blocks(
        attend_backward, (query_w, keyval_w, attention_w, context_grad_w), block_size
    )
    query_grad = (
        window_grid(query_grad_w, depth_count, height_count, width_count)
        .astype(jnp.bfloat16)
        .reshape(-1, C)
    )
    _, spread_back = jax.vjp(
        lambda region: gather_search(region, depth_count, height_count, width_count),
        jnp.zeros(partner_keyval.shape, jnp.float32),
    )
    region_grad = spread_back(keyval_grad_w)[0][:, :, 1:-1]
    folded = fold_rims(region_grad.reshape(depth_len + 2, height_len + 2, width_len * 2 * C))
    partner_grad = folded.astype(jnp.bfloat16)
    query_wgrad = jnp.dot(normal_rows.T, query_grad, preferred_element_type=jnp.float32)
    own_keyval_grad = from_partner(partner_grad, "stream", 0).reshape(-1, 2 * C)
    keyval_wgrad = jnp.dot(normal_rows.T, own_keyval_grad, preferred_element_type=jnp.float32)
    norm_grad = jnp.dot(query_grad, w_query.T, preferred_element_type=jnp.float32) + jnp.dot(
        own_keyval_grad, w_keyval.T, preferred_element_type=jnp.float32
    )
    norm_grad = norm_grad.reshape(values.shape)
    gain_part = jnp.sum((norm_grad * normed).reshape(-1, C), 0)
    token_grad = (
        normalize_back(values, norm_grad * ln_gain)
        + output_grad.reshape(values.shape).astype(jnp.float32)
    ).astype(jnp.bfloat16)
    device_total = lax.axis_size("stream") * lax.axis_size("depth") * lax.axis_size("height")
    grad_scale = (1.0 * device_total * depth_len * height_len * width_len) ** (-0.5)
    summed = lax.psum(
        (gain_part, query_wgrad, keyval_wgrad, out_wgrad, merge_wgrad),
        ("stream", "depth", "height"),
    )
    return (
        relayed[None],
        token_grad.reshape(tokens.shape),
        summed[0] * grad_scale,
        summed[1] * grad_scale,
        summed[2] * grad_scale,
        summed[3] * grad_scale,
        summed[4] * grad_scale,
    )


def solution(mesh):
    in_specs = (
        P("stream", "depth", "height", None),
        P(),
        P(),
        P(),
        P(),
        P(),
        P("depth", "height"),
        P("stream", ("depth", "height"), None),
    )
    out_specs = (
        P("stream", ("depth", "height"), None),
        P("stream", "depth", "height", None),
        P(),
        P(),
        P(),
        P(),
        P(),
    )
    return jax.shard_map(local, mesh=mesh, in_specs=in_specs, out_specs=out_specs, check_vma=False)
```

profile of v0, /device:TPU:1, one launch (start us, length us, event | category | flops | bytes accessed | tf_op | source)
XLA Modules:
  0.0 825.1 jit_solution(7365021637799642939)
XLA Ops:
  23.0 9.8 %collective-permute-start.1 = (s32[1]{0:T(128)}, s32[1]{0:T(128)}, u32[]{:S(2)}, u32[]{:S(2)}) collective-permute-start(s32[1]{0:T(128)} %bitcast.5), channel_id=1, source_target_pairs={{1,0},{2,1},{3,2},{4,3},{5,4},{6,5},{7,6},{8,7},{9,8},{10,9},{11,1... | collective-permute-start | bytes 20 | tf_op jit(solution)/shard_map/ppermute | solution.py:46
  57.0 9.6 %collective-permute-start.10 = (bf16[1,48000]{1,0:T(2,128)(2,1)S(1)}, bf16[1,48000]{1,0:T(2,128)(2,1)S(1)}, u32[]{:S(2)}, u32[]{:S(2)}) collective-permute-start(bf16[1,48000]{1,0:T(2,128)(2,1)S(1)} %get-tuple-element.84), channel_id=1, source_target_pairs={{1,0},{2,1},{3,2},{4,3},{5,4},{6,5},{7,6},{8,7},{9,8},{10,9},{11,1... | collective-permute-start | bytes 288008 | tf_op jit(solution)/shard_map/ppermute | solution.py:46
  67.2 6.9 collective-permute-done.10
  74.1 10.2 %collective-permute-done.9 = bf16[1,48000]{1,0:T(2,128)(2,1)S(1)} collective-permute-done((bf16[1,48000]{1,0:T(2,128)(2,1)S(1)}, bf16[1,48000]{1,0:T(2,128)(2,1)S(1)}, u32[]{:S(2)}, u32[]{:S(2)}) %collective-permute-start.9) | collective-permute-done | bytes 96032 | tf_op jit(solution)/shard_map/ppermute | solution.py:46
  103.5 4.8 collective-permute-start.5
  135.8 4.0 maximum_bitcast_fusion
  143.3 5.5 squeeze.42
  148.8 3.9 fusion.46
  157.6 4.0 fusion.4
  165.6 5.7 fusion.55
  174.3 12.6 %fusion.8 = f32[8,343,6,32]{1,3,2,0:T(8,128)} fusion(bf16[8,125,6,32]{1,3,2,0:T(8,128)(2,1)S(1)} %copy-done.18, bf16[8,6,125,343]{2,3,1,0:T(8,128)(2,1)} %copy-done.1, f32[8,6,125,343]{2,3,1,0:T(8,128)} %fusion.55), kind=kOutput, calls=%fused_computation.22 | convolution fusion | flops 146124336 | bytes 14839392 | tf_op jit(solution)/shard_map/while/body/eval_jaxpr/nhqk,nqhd->nkhd/dot_general | solution.py:188
  186.9 5.0 pad_maximum_fusion
  191.9 20.3 %copy.177 = f32[8,343,12,32]{3,2,0,1:T(8,128)} copy(f32[8,343,12,32]{1,3,2,0:T(8,128)} %pad_maximum_fusion) | data formatting | bytes 8429568 | tf_op jit(solution)/shard_map/while/body/eval_jaxpr/concatenate | solution.py:193
  212.1 16.9 %reshape_reshape.38 = f32[2,2,2,7,7,7,384]{6,2,1,0,5,4,3:T(2,128)} reshape(f32[8,343,12,32]{3,2,0,1:T(8,128)} %copy.177) | data formatting | bytes 8429568 | tf_op jit(solution)/shard_map/transpose(jvp())/reshape;reshape | solution.py:83
  238.1 62.1 %pad.32 = f32[12,2,7,2,7,384]{5,0,3,1,4,2:T(8,128)} pad(f32[2,2,7,2,7,384]{5,0,3,1,4,2:T(2,128)S(1)} %get-tuple-element.56, f32[]{:T(128)} %constant.112.clone.1), padding=6_0_4x0_0_0x0_0_0x0_0_0x0_0_0x0_0_0 | pad | bytes 4214788 | tf_op jit(solution)/shard_map/transpose(jvp())/pad | solution.py:72
  300.2 62.1 %pad.33 = f32[12,2,7,2,7,384]{5,0,3,1,4,2:T(8,128)} pad(f32[2,2,7,2,7,384]{5,0,3,1,4,2:T(2,128)S(1)} %get-tuple-element.55, f32[]{:T(128)} %constant.112.clone.1), padding=0_6_4x0_0_0x0_0_0x0_0_0x0_0_0x0_0_0 | pad | bytes 4214788 | tf_op jit(solution)/shard_map/transpose(jvp())/pad | solution.py:71
  362.4 6.6 add_bitcast_fusion
  373.6 10.4 %pad.35 = f32[12,2,7,12,384]{4,3,0,1,2:T(8,128)} pad(f32[2,2,7,12,384]{4,3,0,1,2:T(8,128)S(1)} %get-tuple-element.54, f32[]{:T(128)} %constant.112.clone.1), padding=6_0_4x0_0_0x0_0_0x0_0_0x0_0_0 | pad | bytes 3612676 | tf_op jit(solution)/shard_map/transpose(jvp())/pad | solution.py:72
  384.0 10.4 %pad.36 = f32[12,2,7,12,384]{4,3,0,1,2:T(8,128)} pad(f32[2,2,7,12,384]{4,3,0,1,2:T(8,128)S(1)} %get-tuple-element.53, f32[]{:T(128)} %constant.112.clone.1), padding=0_6_4x0_0_0x0_0_0x0_0_0x0_0_0 | pad | bytes 3612676 | tf_op jit(solution)/shard_map/transpose(jvp())/pad | solution.py:71
  394.5 5.1 add_bitcast_fusion.1
  418.9 13.2 %pad.153 = f32[12,12,12,384]{3,2,1,0:T(8,128)} pad(f32[2,12,12,384]{3,2,1,0:T(8,128)} %get-tuple-element.57, f32[]{:T(128)} %constant.112.clone.1), padding=0_6_4x0_0_0x0_0_0x0_0_0 | pad | bytes 3096580
  432.2 9.1 %pad.152 = f32[12,12,12,384]{3,2,1,0:T(8,128)} pad(f32[2,12,12,384]{3,2,1,0:T(8,128)S(1)} %copy-done.14, f32[]{:T(128)} %constant.112.clone.1), padding=6_0_4x0_0_0x0_0_0x0_0_0 | pad | bytes 3096580
  441.2 6.7 pad_add_fusion
  447.9 4.5 reshape.458
  459.8 12.1 %fusion.12 = bf16[8,125,6,32]{1,3,2,0:T(8,128)(2,1)} fusion(bf16[8,343,6,32]{1,3,2,0:T(8,128)(2,1)S(1)} %bitcast.155, bf16[8,6,125,343]{2,3,1,0:T(8,128)(2,1)} %copy-done.1, f32[8,6,125,343]{2,3,1,0:T(8,128)} %fusion.55), kind=kOutput, calls=%fused_computation.43 | convolution fusion | flops 146316336 | bytes 13785696 | tf_op jit(solution)/shard_map/while/body/eval_jaxpr/nhqk,nkhd->nqhd/dot_general | solution.py:185
  473.9 4.8 copy.173
  499.7 5.7 collective-permute-start.15
  526.7 4.4 multiply_convert_fusion
  540.8 5.1 collective-permute-done.8
  545.9 7.4 collective-permute-done.7
  554.7 88.6 %psum.35 = f32[192]{0:T(256)S(1)} all-reduce(f32[192]{0:T(256)S(1)} %get-tuple-element.39), channel_id=1, replica_groups=mesh['stream'=2,'depth'=4,'height'=32] {'stream','depth','height'}, use_global_device_ids=true, to_apply=%region_8.9 | all-reduce | flops 192 | bytes 1536 | tf_op jit(solution)/shard_map/psum | solution.py:358
  643.9 165.9 %all-reduce.13.cloned.1.call-done = (f32[192,192]{1,0:T(8,128)}, f32[192,384]{1,0:T(8,128)}, f32[192,192]{1,0:T(8,128)}, f32[1536,384]{1,0:T(8,128)}) async-done(((f32[192,192]{1,0:T(8,128)}, f32[192,384]{1,0:T(8,128)}, f32[192,192]{1,0:T(8,128)}, f32[1536,384]{1,0:T(8,128)}), (f32[192,192]{1,0:T(8,128)}, f32[192,384]{1,0:T(8,128)}, f32[192,192]{1,0:T(8,128)}, ...) | async-done | bytes 2949136 | tf_op jit(solution)/shard_map/psum | solution.py:358
  (262 shorter events, 205.4 us)
Async XLA Ops:
  7.2 78.9 %copy-start = (bf16[1536,384]{1,0:T(8,128)(2,1)S(1)}, bf16[1536,384]{1,0:T(8,128)(2,1)}, u32[]{:S(2)}) copy-start(bf16[1536,384]{1,0:T(8,128)(2,1)} %param.13) | copy-start | bytes 3538948
  7.2 802.7 %all-reduce.13.cloned.1.call-start = ((), (), s32[]{:S(2)}) async-start(), calls=%async_computation | async-start | bytes 6094848 | tf_op jit(solution)/shard_map/psum | solution.py:358
  16.0 22.2 %copy-start.28 = (f32[1000]{0:T(1024)}, f32[1000]{0:T(1024)S(1)}, u32[]{:S(2)}) copy-start(f32[1000]{0:T(1024)S(1)} %rsqrt.14) | copy-start | bytes 12004
  18.5 19.7 %copy-start.25 = (bf16[192,192]{1,0:T(8,128)(2,1)S(1)}, bf16[192,192]{1,0:T(8,128)(2,1)}, u32[]{:S(2)}) copy-start(bf16[192,192]{1,0:T(8,128)(2,1)} %param.10) | copy-start | bytes 221188
  18.5 68.5 %collective-permute-start.2 = (bf16[10,10,3840]{2,1,0:T(8,128)(2,1)}, bf16[10,10,3840]{2,1,0:T(8,128)(2,1)}, u32[]{:S(2)}, u32[]{:S(2)}) collective-permute-start(bf16[10,10,3840]{2,1,0:T(8,128)(2,1)} %reshape.442), channel_id=1, source_target_pairs={{0,128},{128,0},{1,129},{129,1},{2,130},{130,2},{3,131},{131,3},{4... | collective-permute-start | bytes 2304008 | tf_op jit(solution)/shard_map/ppermute | solution.py:27
  23.0 31.1 %collective-permute-start.1 = (s32[1]{0:T(128)}, s32[1]{0:T(128)}, u32[]{:S(2)}, u32[]{:S(2)}) collective-permute-start(s32[1]{0:T(128)} %bitcast.5), channel_id=1, source_target_pairs={{1,0},{2,1},{3,2},{4,3},{5,4},{6,5},{7,6},{8,7},{9,8},{10,9},{11,1... | collective-permute-start | bytes 20 | tf_op jit(solution)/shard_map/ppermute | solution.py:46
  32.8 21.3 %collective-permute-start = (s32[1]{0:T(128)}, s32[1]{0:T(128)}, u32[]{:S(2)}, u32[]{:S(2)}) collective-permute-start(s32[1]{0:T(128)} %bitcast.3), channel_id=1, source_target_pairs={{31,0},{0,1},{1,2},{2,3},{3,4},{4,5},{5,6},{6,7},{7,8},{8,9},{9,10... | collective-permute-start | bytes 20 | tf_op jit(solution)/shard_map/ppermute | solution.py:46
  56.0 29.4 %copy-start.33 = (pred[3]{0:T(512)(128)(4,1)}, pred[3]{0:T(512)(128)(4,1)S(1)}, u32[]{:S(2)}) copy-start(pred[3]{0:T(512)(128)(4,1)S(1)} %add_compare_fusion) | copy-start | bytes 13
  56.2 29.2 %copy-start.35 = (s32[3]{0:T(128)}, s32[3]{0:T(128)S(1)}, u32[]{:S(2)}) copy-start(s32[3]{0:T(128)S(1)} %convert_reduce_fusion) | copy-start | bytes 40
  57.0 17.1 %collective-permute-start.10 = (bf16[1,48000]{1,0:T(2,128)(2,1)S(1)}, bf16[1,48000]{1,0:T(2,128)(2,1)S(1)}, u32[]{:S(2)}, u32[]{:S(2)}) collective-permute-start(bf16[1,48000]{1,0:T(2,128)(2,1)S(1)} %get-tuple-element.84), channel_id=1, source_target_pairs={{1,0},{2,1},{3,2},{4,3},{5,4},{6,5},{7,6},{8,7},{9,8},{10,9},{11,1... | collective-permute-start | bytes 288008 | tf_op jit(solution)/shard_map/ppermute | solution.py:46
  66.7 17.6 %collective-permute-start.9 = (bf16[1,48000]{1,0:T(2,128)(2,1)S(1)}, bf16[1,48000]{1,0:T(2,128)(2,1)S(1)}, u32[]{:S(2)}, u32[]{:S(2)}) collective-permute-start(bf16[1,48000]{1,0:T(2,128)(2,1)S(1)} %get-tuple-element.83), channel_id=1, source_target_pairs={{31,0},{0,1},{1,2},{2,3},{3,4},{4,5},{5,6},{6,7},{7,8},{8,9},{9,10... | collective-permute-start | bytes 288008 | tf_op jit(solution)/shard_map/ppermute | solution.py:46
  88.7 6.8 collective-permute-start.3
  94.0 15.4 %copy-start.5 = (bf16[1000,192]{1,0:T(8,128)(2,1)}, bf16[1000,192]{1,0:T(8,128)(2,1)S(1)}, u32[]{:S(2)}) copy-start(bf16[1000,192]{1,0:T(8,128)(2,1)S(1)} %reshape_reshape.36) | copy-start | bytes 1152004
  94.0 14.3 %copy-start.23 = (bf16[192,192]{1,0:T(8,128)(2,1)S(1)}, bf16[192,192]{1,0:T(8,128)(2,1)}, u32[]{:S(2)}) copy-start(bf16[192,192]{1,0:T(8,128)(2,1)} %param.12) | copy-start | bytes 221188
  94.1 6.0 collective-permute-start.4
  102.2 15.6 %collective-permute-start.6 = (bf16[12,1,3840]{2,1,0:T(2,128)(2,1)}, bf16[12,1,3840]{2,1,0:T(2,128)(2,1)}, u32[]{:S(2)}, u32[]{:S(2)}) collective-permute-start(bf16[12,1,3840]{2,1,0:T(2,128)(2,1)} %get-tuple-element.78), channel_id=1, source_target_pairs={{1,0},{2,1},{3,2},{4,3},{5,4},{6,5},{7,6},{8,7},{9,8},{10,9},{11,1... | collective-permute-start | bytes 276488 | tf_op jit(solution)/shard_map/ppermute | solution.py:38
  103.5 14.4 %collective-permute-start.5 = (bf16[12,1,3840]{2,1,0:T(2,128)(2,1)}, bf16[12,1,3840]{2,1,0:T(2,128)(2,1)}, u32[]{:S(2)}, u32[]{:S(2)}) collective-permute-start(bf16[12,1,3840]{2,1,0:T(2,128)(2,1)} %get-tuple-element.77), channel_id=1, source_target_pairs={{0,1},{1,2},{2,3},{3,4},{4,5},{5,6},{6,7},{7,8},{8,9},{9,10},{10,1... | collective-permute-start | bytes 276488 | tf_op jit(solution)/shard_map/ppermute | solution.py:35
  418.9 13.2 %copy-start.14 = (f32[2,12,12,384]{3,2,1,0:T(8,128)S(1)}, f32[2,12,12,384]{3,2,1,0:T(8,128)}, u32[]{:S(2)}) copy-start(f32[2,12,12,384]{3,2,1,0:T(8,128)} %get-tuple-element.58) | copy-start | bytes 1327108
  455.6 33.5 %collective-permute-start.11 = (bf16[12,1,3840]{2,1,0:T(2,128)(2,1)}, bf16[12,1,3840]{2,1,0:T(2,128)(2,1)}, u32[]{:S(2)}, u32[]{:S(2)}) collective-permute-start(bf16[12,1,3840]{2,1,0:T(2,128)(2,1)} %get-tuple-element.75), channel_id=1, source_target_pairs={{0,1},{1,2},{2,3},{3,4},{4,5},{5,6},{6,7},{7,8},{8,9},{9,10},{10,1... | collective-permute-start | bytes 276488 | tf_op jit(solution)/shard_map/ppermute | solution.py:19
  457.5 31.6 %collective-permute-start.12 = (bf16[12,1,3840]{2,1,0:T(2,128)(2,1)}, bf16[12,1,3840]{2,1,0:T(2,128)(2,1)}, u32[]{:S(2)}, u32[]{:S(2)}) collective-permute-start(bf16[12,1,3840]{2,1,0:T(2,128)(2,1)} %get-tuple-element.76), channel_id=1, source_target_pairs={{1,0},{2,1},{3,2},{4,3},{5,4},{6,5},{7,6},{8,7},{9,8},{10,9},{11,1... | collective-permute-start | bytes 276488 | tf_op jit(solution)/shard_map/ppermute | solution.py:19
  492.0 3.7 collective-permute-start.13
  493.8 5.6 collective-permute-start.14
  495.7 9.7 %copy-start.6 = (bf16[1000,192]{1,0:T(8,128)(2,1)S(1)}, bf16[1000,192]{1,0:T(8,128)(2,1)}, u32[]{:S(2)}) copy-start(bf16[1000,192]{1,0:T(8,128)(2,1)} %copy-done.5) | copy-start | bytes 1152004
  495.7 9.7 %copy-start.8 = (bf16[1000,192]{1,0:T(8,128)(2,1)S(1)}, bf16[1000,192]{1,0:T(8,128)(2,1)}, u32[]{:S(2)}) copy-start(bf16[1000,192]{1,0:T(8,128)(2,1)} %copy-done.7) | copy-start | bytes 1152004
  495.7 10.7 %copy-start.15 = (bf16[1000,192]{1,0:T(8,128)(2,1)S(1)}, bf16[1000,192]{1,0:T(8,128)(2,1)}, u32[]{:S(2)}) copy-start(bf16[1000,192]{1,0:T(8,128)(2,1)} %convert_element_type.219) | copy-start | bytes 1152004
  495.8 10.7 %copy-start.26 = (bf16[192,192]{1,0:T(8,128)(2,1)S(1)}, bf16[192,192]{1,0:T(8,128)(2,1)}, u32[]{:S(2)}) copy-start(bf16[192,192]{1,0:T(8,128)(2,1)} %param.10) | copy-start | bytes 221188
  499.5 8.2 copy-start.11
  499.7 9.9 %collective-permute-start.15 = (bf16[10,10,3840]{2,1,0:T(8,128)(2,1)S(1)}, bf16[10,10,3840]{2,1,0:T(8,128)(2,1)}, u32[]{:S(2)}, u32[]{:S(2)}) collective-permute-start(bf16[10,10,3840]{2,1,0:T(8,128)(2,1)S(1)} %pad_maximum_fusion.3), channel_id=1, source_target_pairs={{0,128},{128,0},{1,129},{129,1},{2,130},{130,2},{3,131},{131,3},{4... | collective-permute-start | bytes 2304008 | tf_op jit(solution)/shard_map/ppermute | solution.py:27
  536.9 16.4 %copy-start.34 = (pred[3]{0:T(512)(128)(4,1)S(1)}, pred[3]{0:T(512)(128)(4,1)}, u32[]{:S(2)}) copy-start(pred[3]{0:T(512)(128)(4,1)} %copy-done.33) | copy-start | bytes 13
  536.9 16.4 %copy-start.36 = (s32[3]{0:T(128)S(1)}, s32[3]{0:T(128)}, u32[]{:S(2)}) copy-start(s32[3]{0:T(128)} %copy-done.35) | copy-start | bytes 40
  538.3 7.6 collective-permute-start.8
  539.0 14.2 %collective-permute-start.7 = (bf16[1,48000]{1,0:T(2,128)(2,1)S(1)}, bf16[1,48000]{1,0:T(2,128)(2,1)S(1)}, u32[]{:S(2)}, u32[]{:S(2)}) collective-permute-start(bf16[1,48000]{1,0:T(2,128)(2,1)S(1)} %get-tuple-element.86), channel_id=1, source_target_pairs={{31,0},{0,1},{1,2},{2,3},{3,4},{4,5},{5,6},{6,7},{7,8},{8,9},{9,10... | collective-permute-start | bytes 288008 | tf_op jit(solution)/shard_map/ppermute | solution.py:46
  (23 other events, 90.9 us)
Sparse Core Ops, SparseCore 0:
  537.0 272.8 all-reduce.12
where the time goes:
time: 834 us; the launch traced here: 825 us
  local copies, waits for them, and re-layouts  352 us (42%)
  waiting for transfers between devices  201 us (24%)
  blocking collectives  88.6 us (11%)
  other arithmetic  64.9 us (8%)
  matrix products  55.1 us (7%)
  starting transfers between devices  47.5 us (6%)
  between operations  15.9 us (2%)
    psum x1, waiting for transfers between devices, local(): lax.psum((gain_part, query_wgrad, keyval_wgrad, out_wgrad, merge_wgrad),...  166 us
    psum x1, blocking collectives, local(): lax.psum((gain_part, query_wgrad, keyval_wgrad, out_wgrad, merge_wgrad),...  88.6 us
    pad x2, local copies, waits for them, and re-layouts, window_rims(): after_rim = leading[6:number * 5 + 2:5][:, None]  72.6 us
    pad x2, local copies, waits for them, and re-layouts, window_rims(): before = leading[0:number * 5:5][:, None]  72.6 us
    ppermute x6, waiting for transfers between devices, passed_along(): return lax.ppermute(block, axis, route)  29.5 us
    unnamed x80, local copies, waits for them, and re-layouts  27.8 us
    ppermute x6, starting transfers between devices, passed_along(): return lax.ppermute(block, axis, route)  22.1 us
    concatenate x1, local copies, waits for them, and re-layouts, attend_backward(): jnp.concatenate([key_grad, value_grad], 2).reshape(windows, 343, 2 * C)  20.3 us
  transfers between devices with their start and end apart: 17, of which 7 were waited for; matrix products, arithmetic and copies ran while one was open for 10% of the time, Pallas kernels for 0%

commit v1 on v0

v1 whole, which is shorter than its diff:
```python
import functools

import jax
import jax.numpy as jnp
import numpy as np
from jax import lax
from jax.experimental import pallas as pl
from jax.experimental.pallas import tpu as pltpu
from jax.sharding import PartitionSpec as P

C = 192
HEADS = 6
EPS = 1e-05
N_DEPTH = 4
N_HEIGHT = 32
SCALE = 32 ** (-0.5)
EXP2_SCALE = SCALE * 1.4426950408889634
MESH = pl.DeviceIdType.MESH
F32 = jnp.float32
BF16 = jnp.bfloat16
VM = pl.BlockSpec(memory_space=pltpu.VMEM)
SM = pl.BlockSpec(memory_space=pltpu.SMEM)
LIMIT = 56 * 1024 * 1024


def dot(a, b):
    return lax.dot_general(a, b, (((1,), (0,)), ((), ())), preferred_element_type=F32)


def dot_nt(a, b):
    return lax.dot_general(a, b, (((1,), (1,)), ((), ())), preferred_element_type=F32)


def dot_tn(a, b):
    return lax.dot_general(a, b, (((0,), (0,)), ((), ())), preferred_element_type=F32)


def place():
    return lax.axis_index("stream"), lax.axis_index("depth"), lax.axis_index("height")


def neighbours():
    s, d, h = place()
    dl, dh = lax.rem(d + N_DEPTH - 1, N_DEPTH), lax.rem(d + 1, N_DEPTH)
    hl, hh = lax.rem(h + N_HEIGHT - 1, N_HEIGHT), lax.rem(h + 1, N_HEIGHT)
    o = 1 - s
    return {
        "p": (o, d, h),
        "dl": (o, dl, h),
        "dh": (o, dh, h),
        "hl": (o, d, hl),
        "hh": (o, d, hh),
        "ll": (o, dl, hl),
        "lh": (o, dl, hh),
        "hdl": (o, dh, hl),
        "hdh": (o, dh, hh),
        "sl": (s, d, hl),
        "sh": (s, d, hh),
    }


def greet(peers):
    barrier = pltpu.get_barrier_semaphore()
    for peer in peers:
        pl.semaphore_signal(barrier, inc=1, device_id=peer, device_id_type=MESH)
    pl.semaphore_wait(barrier, len(peers))


def copier(send_sem, recv_sem):
    def make(src, dst, index, peer):
        return pltpu.make_async_remote_copy(
            src_ref=src,
            dst_ref=dst,
            send_sem=send_sem.at[index],
            recv_sem=recv_sem.at[index],
            device_id=peer,
            device_id_type=MESH,
        )

    return make


def relay_ranks(fl, fs, fr):
    _, _, h = place()
    left, right = lax.rem(h + N_HEIGHT - 1, N_HEIGHT), lax.rem(h + 1, N_HEIGHT)

    def before(a, b):
        return jnp.where(a < b, 1, 0)

    rank_l = fs * before(h, left) + fr * before(right, left)
    rank_s = fl * before(left, h) + fr * before(right, h)
    rank_r = fl * before(left, right) + fs * before(h, right)
    return rank_l, rank_s, rank_r


def wide(row):
    return jnp.concatenate([row, row, row], axis=1)


def intake_kernel(
    tok, rg, own, own_tok, region, rims, corners, merged_grad, owners,
    stage, hstage, hsend, rows, mg_send, mg_recv, own_send, send_sem, recv_sem,
):
    _, _, h = place()
    peers = neighbours()
    copy = copier(send_sem, recv_sem)
    own_send[...] = jnp.full((8, 128), own[0, 0], jnp.int32)
    greet(list(peers.values()))
    to_left = copy(own_send, owners.at[2], 0, peers["sl"])
    to_right = copy(own_send, owners.at[0], 1, peers["sh"])
    to_left.start()
    to_right.start()
    owners[1] = own_send[...]
    stage[...] = jnp.zeros_like(stage)
    hstage[...] = jnp.zeros_like(hstage)
    for d in range(10):
        x = tok[d].astype(F32)
        stage[d, 1:7, :] = x[0:6]
        stage[d, 9:14, :] = x[5:10]
        stage[d, 8:9, :] = x[4:5]
        hstage[0, d : d + 1, :] = x[0:1]
        hstage[1, d : d + 1, :] = x[9:10]
    own_tok[...] = stage[...].astype(BF16)
    hsend[...] = hstage[...].astype(BF16)
    copies = [
        copy(own_tok, region.at[pl.ds(1, 10)], 2, peers["p"]),
        copy(own_tok.at[9], region.at[0], 3, peers["dh"]),
        copy(own_tok.at[0], region.at[11], 4, peers["dl"]),
        copy(hsend.at[1], rims.at[0], 5, peers["hh"]),
        copy(hsend.at[0], rims.at[1], 6, peers["hl"]),
        copy(own_tok.at[9], corners.at[0], 7, peers["hdh"]),
        copy(own_tok.at[9], corners.at[1], 8, peers["hdl"]),
        copy(own_tok.at[0], corners.at[2], 9, peers["lh"]),
        copy(own_tok.at[0], corners.at[3], 10, peers["ll"]),
    ]
    for one in copies:
        one.start()
    rows[...] = jnp.zeros_like(rows)

    def spread(i, carry):
        x = rg[:, pl.ds(pl.multiple_of(i * 384, 128), 384)].astype(F32)
        for k in range(3):
            rows[k, pl.ds(i, 1), :] = x[k : k + 1]
        return carry

    lax.fori_loop(0, 125, spread, 0)
    to_left.wait()
    to_right.wait()
    fl = jnp.where(owners[0, 0:1, :] == h, 1, 0)
    fs = jnp.where(owners[1, 0:1, :] == h, 1, 0)
    fr = jnp.where(owners[2, 0:1, :] == h, 1, 0)
    rank_l, rank_s, rank_r = relay_ranks(fl, fs, fr)

    def pick(rank):
        rank = wide(rank)
        return jnp.where(rank == 0, rows[0], jnp.where(rank == 1, rows[1], rows[2]))

    mg_send[0] = pick(rank_l).astype(BF16)
    mg_send[1] = pick(rank_r).astype(BF16)
    back_left = copy(mg_send.at[0], mg_recv.at[1], 11, peers["sl"])
    back_right = copy(mg_send.at[1], mg_recv.at[0], 12, peers["sh"])
    back_left.start()
    back_right.start()
    mine = pick(rank_s)
    left, right = lax.rem(h + N_HEIGHT - 1, N_HEIGHT), lax.rem(h + 1, N_HEIGHT)
    target = wide(owners[1, 0:1, :])
    back_left.wait()
    back_right.wait()
    merged_grad[...] = jnp.where(
        target == left,
        mg_recv[0].astype(F32),
        jnp.where(target == right, mg_recv[1].astype(F32), mine),
    ).astype(BF16)
    for one in copies:
        one.wait()


def intake(tok, rg, own):
    return pl.pallas_call(
        intake_kernel,
        out_shape=(
            jax.ShapeDtypeStruct((10, 16, 1920), BF16),
            jax.ShapeDtypeStruct((12, 16, 1920), BF16),
            jax.ShapeDtypeStruct((2, 16, 1920), BF16),
            jax.ShapeDtypeStruct((4, 16, 1920), BF16),
            jax.ShapeDtypeStruct((128, 384), BF16),
            jax.ShapeDtypeStruct((3, 8, 128), jnp.int32),
        ),
        in_specs=[VM, VM, SM],
        out_specs=(VM,) * 6,
        scratch_shapes=[
            pltpu.VMEM((10, 16, 1920), F32),
            pltpu.VMEM((2, 16, 1920), F32),
            pltpu.VMEM((2, 16, 1920), BF16),
            pltpu.VMEM((3, 128, 384), F32),
            pltpu.VMEM((2, 128, 384), BF16),
            pltpu.VMEM((2, 128, 384), BF16),
            pltpu.VMEM((8, 128), jnp.int32),
            pltpu.SemaphoreType.DMA((13,)),
            pltpu.SemaphoreType.DMA((13,)),
        ],
        compiler_params=pltpu.CompilerParams(
            collective_id=1, has_side_effects=True, vmem_limit_bytes=LIMIT
        ),
        name="intake",
    )(tok, rg, own)


def normalized(x):
    centre = jnp.mean(x, -1, keepdims=True)
    shifted = x - centre
    inverse = lax.rsqrt(jnp.mean(shifted * shifted, -1, keepdims=True) + EPS)
    return shifted * inverse, inverse


def eight_index(window, q):
    wi, di, hi = window // 4, (window // 2) % 2, window % 2
    a = (q * 41) >> 10
    rest = q - a * 25
    b = (rest * 205) >> 10
    c = rest - b * 5
    w, d, h = a + 5 * wi, b + 5 * di, c + 5 * hi
    offset = ((d & 1) * 2 + (h & 1)) * 2 + (w & 1)
    cell = ((d >> 1) * 5 + (h >> 1)) * 5 + (w >> 1)
    return jnp.where(q < 125, offset * 128 + cell, -1)


def compute_kernel(
    own_tok, region, rims, corners, mg, gain, wq, wkv, wo, wm, g, gt,
    merged, gm, go, qg_n, og_n, kv_main, kv_d, kv_h, kv_c,
    reg, qreg, xreg, kreg, vreg, acck, accv, og_e, out_w, pt, qbd, qbd_t, cgbd, cgbd_t,
    ctx_t, qg_t, cstage, wk, wv,
):
    _, dep, hei = place()
    slot = lax.broadcasted_iota(jnp.int32, (16, 1920), 0)
    for d in range(12):
        v = region[d].astype(F32)
        if d == 0:
            lo, hi = corners[0].astype(F32)[13:14], corners[1].astype(F32)[1:2]
        elif d == 11:
            lo, hi = corners[2].astype(F32)[13:14], corners[3].astype(F32)[1:2]
        else:
            lo = rims[0].astype(F32)[d - 1 : d]
            hi = rims[1].astype(F32)[d - 1 : d]
        reg[d] = jnp.where(slot == 0, lo, jnp.where(slot == 14, hi, v))
    row = lax.broadcasted_iota(jnp.int32, (192, 256), 0)
    lane = lax.broadcasted_iota(jnp.int32, (192, 256), 1)
    rd, rs = row >> 4, row & 15
    outside = (
        ((rd == 0) & (dep == 0))
        | ((rd == 11) & (dep == N_DEPTH - 1))
        | ((rs == 0) & (hei == 0))
        | ((rs == 14) & (hei == N_HEIGHT - 1))
        | ((rs & 7) == 7)
    )
    bias = jnp.where(outside & (lane == 192), -1e30, 0.0)
    edge = jnp.where(lane == 192, -1e30, 0.0).reshape(12, 16, 256)
    gains = gain[...]
    wk[...] = jnp.zeros_like(wk)
    wk[:, :C] = wkv[:, :C]
    wv[...] = wkv[:, C:]
    for pair in range(5):
        lanes = slice(384 * pair, 384 * pair + 384)
        own2 = own_tok[:, :, lanes].astype(F32).reshape(160, 384)
        reg2 = reg[:, :, lanes].reshape(192, 384)
        for half in range(2):
            w = 2 * pair + half
            x = own2[:, 192 * half : 192 * half + 192]
            normal = (normalized(x)[0] * gains).astype(BF16)
            qreg[w] = dot(normal, wq[...]).reshape(10, 16, C)
            xreg[w] = x.reshape(10, 16, C)
            y = reg2[:, 192 * half : 192 * half + 192]
            normal = (normalized(y)[0] * gains).astype(BF16)
            kreg[w + 1] = (dot(normal, wk[...]) + bias).reshape(12, 16, 256)
            vreg[w + 1] = dot(normal, wv[...]).reshape(12, 16, C)
    for w in (0, 11):
        kreg[w] = edge
        vreg[w] = jnp.zeros((12, 16, C), F32)
    acck[...] = jnp.zeros_like(acck)
    accv[...] = jnp.zeros_like(accv)
    for o in range(8):
        og_e[128 * o : 128 * o + 128, :] = dot_nt(
            mg[...], wm[192 * o : 192 * o + 192, :]
        ).astype(BF16)
    qbd_t[...] = jnp.zeros_like(qbd_t)
    cgbd_t[...] = jnp.zeros_like(cgbd_t)
    ones = lax.broadcasted_iota(jnp.int32, (64, 768), 0)
    qbd_t[192:256, :] = jnp.where(ones == 0, 1.0, 0.0).astype(BF16)
    go[...] = jnp.zeros_like(go)
    head = lax.broadcasted_iota(jnp.int32, (128, C), 1) >> 5

    def window(i, carry):
        wi, di, hi = i // 4, (i // 2) % 2, i % 2
        hs = pl.ds(pl.multiple_of(hi * 8, 8), 8)
        cells = (pl.ds(wi * 5, 5), pl.ds(di * 5 + 0, 5), hs)
        around = (pl.ds(wi * 5, 7), pl.ds(di * 5, 7), hs)
        q_w = dot(gt[...], qreg[(*cells, slice(None))].reshape(200, C).astype(BF16))
        x_w = dot(gt[...], xreg[(*cells, slice(None))].reshape(200, C).astype(BF16))
        q = lax.broadcasted_iota(jnp.int32, (128, 1024), 0)
        col = lax.broadcasted_iota(jnp.int32, (128, 1024), 1)
        pick = jnp.where(eight_index(i, q) == col, 1.0, 0.0).astype(BF16)
        q = lax.broadcasted_iota(jnp.int32, (1024, 128), 1)
        col = lax.broadcasted_iota(jnp.int32, (1024, 128), 0)
        pt[i] = jnp.where(eight_index(i, q) == col, 1.0, 0.0).astype(BF16)
        og_w = dot(pick, og_e[...])
        og_b = og_w.astype(BF16)
        cg_w = dot_nt(og_b, wo[...]).astype(BF16).astype(F32)
        q_t = q_w.T.astype(BF16)
        cg_t = cg_w.T.astype(BF16)
        for m in range(HEADS):
            r, l = slice(32 * m, 32 * m + 32), slice(128 * m, 128 * m + 128)
            qbd_t[r, l] = q_t[r]
            cgbd_t[r, l] = cg_t[r]
            qbd[l, :] = jnp.where(head == m, q_w, 0.0).astype(BF16)
            cgbd[l, :] = jnp.where(head == m, cg_w, 0.0).astype(BF16)
        k32 = kreg[(*around, slice(None))].reshape(392, 256)
        v32 = vreg[(*around, slice(None))].reshape(392, C)
        k, v = k32.astype(BF16), v32.astype(BF16)
        k_t = k32[:, :C].T.astype(BF16)
        v_t = v32.T.astype(BF16)
        kg = jnp.zeros((392, C), F32)
        vg = jnp.zeros((392, C), F32)
        for p in range(3):
            l = slice(256 * p, 256 * p + 256)
            e = jnp.exp2(dot(k, qbd_t[:, l]) * EXP2_SCALE)
            a = (e * (1.0 / jnp.sum(e, 0, keepdims=True))).astype(BF16)
            af = a.astype(F32)
            c = dot(v_t[64 * p : 64 * p + 64], a)
            ctx_t[64 * p : 64 * p + 32, :] = c[:32, :128]
            ctx_t[64 * p + 32 : 64 * p + 64, :] = c[32:, 128:]
            wg = dot(v, cgbd_t[:, l])
            total = jnp.sum(wg * af, 0, keepdims=True)
            sg = (af * (wg - total) * SCALE).astype(BF16)
            vg = vg + dot(a, cgbd[l, :])
            kg = kg + dot(sg, qbd[l, :])
            c = dot(k_t[64 * p : 64 * p + 64], sg)
            qg_t[64 * p : 64 * p + 32, :] = c[:32, :128]
            qg_t[64 * p + 32 : 64 * p + 64, :] = c[32:, 128:]
        acck[(*around, slice(None))] += kg.reshape(7, 7, 8, C)
        accv[(*around, slice(None))] += vg.reshape(7, 7, 8, C)
        c_t = ctx_t[...]
        go[...] += dot(c_t.astype(BF16), og_b)
        c_w = c_t.T.astype(BF16)
        out_w[pl.ds(pl.multiple_of(i * 128, 128), 128), :] = (dot(c_w, wo[...]) + x_w).astype(BF16)
        qg_w = qg_t[...].T.astype(BF16)
        qg_n[(*cells, slice(None))] = dot(g[...], qg_w).reshape(5, 5, 8, C)
        og_n[(*cells, slice(None))] = dot(g[...], og_b).reshape(5, 5, 8, C)
        return carry

    lax.fori_loop(0, 8, window, 0)
    out_e = dot(pt[0], out_w[0:128, :])
    for i in range(1, 8):
        out_e = out_e + dot(pt[i], out_w[128 * i : 128 * i + 128, :])
    out_b = out_e.astype(BF16)
    total = jnp.zeros((128, 384), F32)
    for o in range(8):
        part = out_b[128 * o : 128 * o + 128]
        total = total + dot(part, wm[192 * o : 192 * o + 192, :])
        gm[192 * o : 192 * o + 192, :] = dot_tn(part, mg[...]).astype(BF16)
    merged[...] = total.astype(BF16)

    slot = lax.broadcasted_iota(jnp.int32, (12, 16, 384), 1)
    inner = (slot & 7 >= 1) & (slot & 7 <= 5)
    srow = lax.broadcasted_iota(jnp.int32, (16, 192), 0)
    scol = lax.broadcasted_iota(jnp.int32, (16, 192), 1)
    low = jnp.where(scol == srow * 16, 1.0, 0.0).astype(BF16)
    high = jnp.where(scol == srow * 16 + 14, 1.0, 0.0).astype(BF16)
    cstage[...] = jnp.zeros_like(cstage)
    for w in range(10):
        t = jnp.concatenate([acck[w + 1], accv[w + 1]], axis=-1)
        flat = t.reshape(192, 384).astype(BF16)
        lo, hi = dot(low, flat), dot(high, flat)
        kv_h[0, w] = lo.astype(BF16)
        kv_h[1, w] = hi.astype(BF16)
        cstage[0, w : w + 1, :] = lo[0:1]
        cstage[1, w : w + 1, :] = hi[0:1]
        cstage[2, w : w + 1, :] = lo[11:12]
        cstage[3, w : w + 1, :] = hi[11:12]
        t = t + jnp.where(slot == 5, t[:, 8:9, :], jnp.where(slot == 9, t[:, 6:7, :], 0.0))
        b = jnp.where(inner, t, 0.0).astype(BF16)
        kv_main[w] = b[1:11]
        kv_d[0, w] = b[0]
        kv_d[1, w] = b[11]
    kv_c[...] = cstage[...].astype(BF16)


def compute(own_tok, region, rims, corners, mg, gain, wq, wkv, wo, wm):
    g = np.zeros((200, 128), np.float32)
    for a in range(5):
        for b in range(5):
            for c in range(5):
                g[(a * 5 + b) * 8 + c + 1, a * 25 + b * 5 + c] = 1
    g = jnp.asarray(g, BF16)
    return pl.pallas_call(
        compute_kernel,
        out_shape=(
            jax.ShapeDtypeStruct((128, 384), BF16),
            jax.ShapeDtypeStruct((1536, 384), BF16),
            jax.ShapeDtypeStruct((C, C), F32),
            jax.ShapeDtypeStruct((10, 10, 16, C), F32),
            jax.ShapeDtypeStruct((10, 10, 16, C), F32),
            jax.ShapeDtypeStruct((10, 10, 16, 384), BF16),
            jax.ShapeDtypeStruct((2, 10, 16, 384), BF16),
            jax.ShapeDtypeStruct((2, 10, 16, 384), BF16),
            jax.ShapeDtypeStruct((4, 16, 384), BF16),
        ),
        in_specs=[VM] * 12,
        out_specs=(VM,) * 9,
        scratch_shapes=[
            pltpu.VMEM((12, 16, 1920), F32),
            pltpu.VMEM((10, 10, 16, C), F32),
            pltpu.VMEM((10, 10, 16, C), F32),
            pltpu.VMEM((12, 12, 16, 256), F32),
            pltpu.VMEM((12, 12, 16, C), F32),
            pltpu.VMEM((12, 12, 16, C), F32),
            pltpu.VMEM((12, 12, 16, C), F32),
            pltpu.VMEM((1024, C), BF16),
            pltpu.VMEM((1024, C), BF16),
            pltpu.VMEM((8, 1024, 128), BF16),
            pltpu.VMEM((768, C), BF16),
            pltpu.VMEM((256, 768), BF16),
            pltpu.VMEM((768, C), BF16),
            pltpu.VMEM((C, 768), BF16),
            pltpu.VMEM((C, 128), F32),
            pltpu.VMEM((C, 128), F32),
            pltpu.VMEM((4, 16, 384), F32),
            pltpu.VMEM((C, 256), BF16),
            pltpu.VMEM((C, C), BF16),
        ],
        compiler_params=pltpu.CompilerParams(vmem_limit_bytes=LIMIT),
        name="compute",
    )(own_tok, region, rims, corners, mg, gain, wq, wkv, wo, wm, g, g.T)


def exchange_kernel(
    main, kd, kh, kc, merged, r_main, r_d, r_h, r_c, r_merged, send_sem, recv_sem
):
    peers = neighbours()
    copy = copier(send_sem, recv_sem)
    greet(list(peers.values()))
    copies = [
        copy(main, r_main, 0, peers["p"]),
        copy(kd.at[0], r_d.at[1], 1, peers["dl"]),
        copy(kd.at[1], r_d.at[0], 2, peers["dh"]),
        copy(kh.at[0], r_h.at[1], 3, peers["hl"]),
        copy(kh.at[1], r_h.at[0], 4, peers["hh"]),
        copy(kc.at[0], r_c.at[3], 5, peers["ll"]),
        copy(kc.at[1], r_c.at[2], 6, peers["lh"]),
        copy(kc.at[2], r_c.at[1], 7, peers["hdl"]),
        copy(kc.at[3], r_c.at[0], 8, peers["hdh"]),
        copy(merged, r_merged.at[1], 9, peers["sl"]),
        copy(merged, r_merged.at[0], 10, peers["sh"]),
    ]
    for one in copies:
        one.start()
    for one in copies:
        one.wait()


def exchange(main, kd, kh, kc, merged):
    return pl.pallas_call(
        exchange_kernel,
        out_shape=(
            jax.ShapeDtypeStruct((10, 10, 16, 384), BF16),
            jax.ShapeDtypeStruct((2, 10, 16, 384), BF16),
            jax.ShapeDtypeStruct((2, 10, 16, 384), BF16),
            jax.ShapeDtypeStruct((4, 16, 384), BF16),
            jax.ShapeDtypeStruct((2, 128, 384), BF16),
        ),
        in_specs=[VM] * 5,
        out_specs=(VM,) * 5,
        scratch_shapes=[pltpu.SemaphoreType.DMA((11,)), pltpu.SemaphoreType.DMA((11,))],
        compiler_params=pltpu.CompilerParams(
            collective_id=2, has_side_effects=True, vmem_limit_bytes=LIMIT
        ),
        name="exchange",
    )(main, kd, kh, kc, merged)


def finish_kernel(
    own_tok, qg, og, main, rd, rh, rc, merged, r_merged, owners, gain, wq, wkv, go,
    token_grad, relayed, small,
    normals, kvs, qgs, stage, stage2, wins, wide_out,
):
    _, _, h = place()
    gains = gain[...]
    slot = lax.broadcasted_iota(jnp.int32, (16, 384), 0)
    gain_sum = jnp.zeros((1, C), F32)
    for pair in range(5):
        lanes = slice(384 * pair, 384 * pair + 384)
        own2 = own_tok[:, :, lanes].astype(F32).reshape(160, 384)
        grads = []
        for half in range(2):
            w = 2 * pair + half
            lo, hi = rh[0, w].astype(F32), rh[1, w].astype(F32)
            planes = []
            for d in range(10):
                lo_d, hi_d = lo[d + 1 : d + 2], hi[d + 1 : d + 2]
                if d == 0:
                    lo_d = lo_d + rc[0].astype(F32)[w : w + 1]
                    hi_d = hi_d + rc[1].astype(F32)[w : w + 1]
                if d == 9:
                    lo_d = lo_d + rc[2].astype(F32)[w : w + 1]
                    hi_d = hi_d + rc[3].astype(F32)[w : w + 1]
                t = main[w, d].astype(F32)
                t = t + jnp.where(slot == 1, lo_d, jnp.where(slot == 13, hi_d, 0.0))
                if d == 0:
                    t = t + rd[0, w].astype(F32)
                if d == 9:
                    t = t + rd[1, w].astype(F32)
                planes.append(t.astype(BF16))
            kv_b = jnp.concatenate(planes, axis=0)
            qg_b = qg[w].reshape(160, C).astype(BF16)
            rows = slice(160 * w, 160 * w + 160)
            kvs[rows, :] = kv_b
            qgs[rows, :] = qg_b
            x = own2[:, 192 * half : 192 * half + 192]
            normed, inverse = normalized(x)
            normals[rows, :] = (normed * gains).astype(BF16)
            ng = dot_nt(qg_b, wq[...]) + dot_nt(kv_b, wkv[...])
            gain_sum = gain_sum + jnp.sum(ng * normed, 0, keepdims=True)
            u = ng * gains
            grads.append(
                inverse
                * (
                    u
                    - jnp.mean(u, -1, keepdims=True)
                    - normed * jnp.mean(u * normed, -1, keepdims=True)
                )
                + og[w].reshape(160, C)
            )
        stage[:, :, lanes] = jnp.concatenate(grads, axis=1).reshape(10, 16, 384)
    for d in range(10):
        x = stage[d]
        stage2[d, 0:5, :] = x[1:6]
        stage2[d, 5:10, :] = x[9:14]
    token_grad[...] = stage2[...].astype(BF16)
    small[...] = jnp.zeros_like(small)
    small[0:192, :] = dot_tn(normals[...], kvs[...]).astype(BF16)
    small[192:384, :] = jnp.concatenate([dot_tn(normals[...], qgs[...]), go[...]], axis=1).astype(
        BF16
    )
    first = lax.broadcasted_iota(jnp.int32, (16, 384), 0)
    spread = jnp.concatenate([gain_sum, jnp.zeros((1, C), F32)], axis=1)
    small[384:400, :] = jnp.where(first == 0, spread, 0.0).astype(BF16)

    fl = jnp.where(owners[0, 0:1, :] == h, 1, 0)
    fs = jnp.where(owners[1, 0:1, :] == h, 1, 0)
    fr = jnp.where(owners[2, 0:1, :] == h, 1, 0)
    ranks = relay_ranks(fl, fs, fr)
    parts = []
    for flag, rank, win in zip((fl, fs, fr), ranks, (r_merged[0], merged[...], r_merged[1])):
        parts.append((wide(jnp.where(flag == 1, rank, -1)), win.astype(F32)))
    for k in range(3):
        total = jnp.zeros((128, 384), F32)
        for key, win in parts:
            total = jnp.where(key == k, win, total)
        wins[k] = total

    def lay(i, carry):
        lanes = pl.ds(pl.multiple_of(i * 384, 128), 384)
        for k in range(3):
            wide_out[k : k + 1, lanes] = wins[k, pl.ds(i, 1), :]
        return carry

    lax.fori_loop(0, 125, lay, 0)
    relayed[...] = wide_out[...].astype(BF16)


def finish(own_tok, qg, og, main, rd, rh, rc, merged, r_merged, owners, gain, wq, wkv, go):
    return pl.pallas_call(
        finish_kernel,
        out_shape=(
            jax.ShapeDtypeStruct((10, 10, 1920), BF16),
            jax.ShapeDtypeStruct((3, 48000), BF16),
            jax.ShapeDtypeStruct((512, 384), BF16),
        ),
        in_specs=[VM] * 14,
        out_specs=(VM,) * 3,
        scratch_shapes=[
            pltpu.VMEM((1600, C), BF16),
            pltpu.VMEM((1600, 384), BF16),
            pltpu.VMEM((1600, C), BF16),
            pltpu.VMEM((10, 16, 1920), F32),
            pltpu.VMEM((10, 10, 1920), F32),
            pltpu.VMEM((3, 128, 384), F32),
            pltpu.VMEM((3, 48000), F32),
        ],
        compiler_params=pltpu.CompilerParams(vmem_limit_bytes=LIMIT),
        name="finish",
    )(own_tok, qg, og, main, rd, rh, rc, merged, r_merged, owners, gain, wq, wkv, go)


def add_up_kernel(
    gm, sm, out_g, out_s,
    acc, snd2, snd3, snd4, fin, acc2, acc3, r1, r2, r3, r4, res2, res3, res4,
    s_send, s_recv, z_send, z_recv,
):
    s, d, h = place()
    zh, xy = h // 16, lax.rem(h, 16)
    x, y = xy // 4, lax.rem(xy, 4)
    z = zh * 4 + d
    partner = (1 - s, d, h)
    xs = [(s, d, zh * 16 + lax.rem(x + k, 4) * 4 + y) for k in (1, 2, 3)]
    ys = [(s, d, zh * 16 + x * 4 + lax.rem(y + k, 4)) for k in (1, 2, 3)]
    xk = [lax.rem(x + k, 4) for k in (1, 2, 3)]
    yk = [lax.rem(y + k, 4) for k in (1, 2, 3)]
    zk = [lax.rem(z + k, 8) for k in range(1, 8)]
    zs = [(s, lax.rem(t, 4), (t // 4) * 16 + xy) for t in zk]
    copy = copier(s_send, s_recv)
    greet([partner] + xs + ys + zs)

    def run(copies):
        for one in copies:
            one.start()
        for one in copies:
            one.wait()

    o = 1 - s
    run([
        copy(gm.at[pl.ds(48 * o, 48)], r1.at[pl.ds(0, 48)], 0, partner),
        copy(sm.at[pl.ds(16 * o, 16)], r1.at[pl.ds(48, 16)], 1, partner),
    ])
    acc[0:48] = gm[pl.ds(48 * s, 48)].astype(F32) + r1[0:48].astype(F32)
    acc[48:64] = sm[pl.ds(16 * s, 16)].astype(F32) + r1[48:64].astype(F32)
    snd2[...] = acc[...].astype(BF16)
    run([
        copy(snd2.at[pl.ds(8 * xk[k], 8)], r2.at[0, k], 2 + k, xs[k]) for k in range(3)
    ] + [
        copy(snd2.at[pl.ds(32 + 8 * yk[k], 8)], r2.at[1, k], 5 + k, ys[k]) for k in range(3)
    ])
    for part, at in ((0, 8 * x), (1, 32 + 8 * y)):
        acc2[pl.ds(8 * part, 8)] = (
            acc[pl.ds(at, 8)]
            + r2[part, 0].astype(F32)
            + r2[part, 1].astype(F32)
            + r2[part, 2].astype(F32)
        )
    snd3[...] = acc2[...].astype(BF16)
    run([
        copy(snd3.at[pl.ds(2 * yk[k], 2)], r3.at[0, k], 8 + k, ys[k]) for k in range(3)
    ] + [
        copy(snd3.at[pl.ds(8 + 2 * xk[k], 2)], r3.at[1, k], 11 + k, xs[k]) for k in range(3)
    ])
    for part, at in ((0, 2 * y), (1, 8 + 2 * x)):
        acc3[pl.ds(2 * part, 2)] = (
            acc2[pl.ds(at, 2)]
            + r3[part, 0].astype(F32)
            + r3[part, 1].astype(F32)
            + r3[part, 2].astype(F32)
        )
    snd4[...] = acc3[...].astype(BF16)
    zcopy = copier(z_send, z_recv)
    for k in range(7):
        owner = zk[k]

        @pl.when(lax.rem(owner, 2) == 0)
        def _():
            zcopy(snd4.at[owner // 2], r4.at[k], k, zs[k]).start()

    @pl.when(lax.rem(z, 2) == 0)
    def _():
        for k in range(7):
            zcopy(snd4.at[0], r4.at[k], k, zs[k]).wait_recv()
        total = acc3[z // 2]
        for k in range(7):
            total = total + r4[k].astype(F32)
        fin[...] = total.astype(BF16)
        res4[z // 2] = fin[...]
        for k in range(7):
            zcopy(fin, res4.at[z // 2], 7 + k, zs[k]).start()

    for k in range(7):
        owner = zk[k]

        @pl.when(lax.rem(owner, 2) == 0)
        def _():
            zcopy(snd4.at[owner // 2], r4.at[k], k, zs[k]).wait_send()
            zcopy(fin, res4.at[owner // 2], 7 + (6 - k), zs[k]).wait_recv()

    @pl.when(lax.rem(z, 2) == 0)
    def _():
        for k in range(7):
            zcopy(fin, res4.at[z // 2], 7 + k, zs[k]).wait_send()

    res3[pl.ds(2 * y, 2)] = res4[0:2]
    res3[pl.ds(8 + 2 * x, 2)] = res4[2:4]
    run([
        copy(res4.at[pl.ds(0, 2)], res3.at[pl.ds(2 * y, 2)], 14 + k, ys[k]) for k in range(3)
    ] + [
        copy(res4.at[pl.ds(2, 2)], res3.at[pl.ds(8 + 2 * x, 2)], 17 + k, xs[k]) for k in range(3)
    ])
    res2[pl.ds(8 * x, 8)] = res3[0:8]
    res2[pl.ds(32 + 8 * y, 8)] = res3[8:16]
    run([
        copy(res3.at[pl.ds(0, 8)], res2.at[pl.ds(8 * x, 8)], 20 + k, xs[k]) for k in range(3)
    ] + [
        copy(res3.at[pl.ds(8, 8)], res2.at[pl.ds(32 + 8 * y, 8)], 23 + k, ys[k]) for k in range(3)
    ])
    out_g[pl.ds(48 * s, 48)] = res2[0:48]
    out_s[pl.ds(16 * s, 16)] = res2[48:64]
    run([
        copy(res2.at[pl.ds(0, 48)], out_g.at[pl.ds(48 * s, 48)], 26, partner),
        copy(res2.at[pl.ds(48, 16)], out_s.at[pl.ds(16 * s, 16)], 27, partner),
    ])


def add_up(gm, sm):
    return pl.pallas_call(
        add_up_kernel,
        out_shape=(
            jax.ShapeDtypeStruct((96, 16, 384), BF16),
            jax.ShapeDtypeStruct((32, 16, 384), BF16),
        ),
        in_specs=[VM] * 2,
        out_specs=(VM,) * 2,
        scratch_shapes=[
            pltpu.VMEM((64, 16, 384), F32),
            pltpu.VMEM((64, 16, 384), BF16),
            pltpu.VMEM((16, 16, 384), BF16),
            pltpu.VMEM((4, 16, 384), BF16),
            pltpu.VMEM((16, 384), BF16),
            pltpu.VMEM((16, 16, 384), F32),
            pltpu.VMEM((4, 16, 384), F32),
            pltpu.VMEM((64, 16, 384), BF16),
            pltpu.VMEM((2, 3, 8, 16, 384), BF16),
            pltpu.VMEM((2, 3, 2, 16, 384), BF16),
            pltpu.VMEM((7, 16, 384), BF16),
            pltpu.VMEM((64, 16, 384), BF16),
            pltpu.VMEM((16, 16, 384), BF16),
            pltpu.VMEM((4, 16, 384), BF16),
            pltpu.SemaphoreType.DMA((28,)),
            pltpu.SemaphoreType.DMA((28,)),
            pltpu.SemaphoreType.DMA((14,)),
            pltpu.SemaphoreType.DMA((14,)),
        ],
        compiler_params=pltpu.CompilerParams(
            collective_id=3, has_side_effects=True, vmem_limit_bytes=LIMIT
        ),
        name="add_up",
    )(gm, sm)


def local(tokens, ln_gain, w_query, w_keyval, w_out, w_merge, owner_map, relay_grad):
    gain = ln_gain.reshape(1, C)
    own_tok, region, rims, corners, mg, owners = intake(tokens[0], relay_grad[0], owner_map)
    merged, gm, go, qg, og, kv_main, kv_d, kv_h, kv_c = compute(
        own_tok, region, rims, corners, mg, gain, w_query, w_keyval, w_out, w_merge
    )
    r_main, r_d, r_h, r_c, r_merged = exchange(kv_main, kv_d, kv_h, kv_c, merged)
    token_grad, relayed, small = finish(
        own_tok, qg, og, r_main, r_d, r_h, r_c, merged, r_merged, owners, gain, w_query,
        w_keyval, go,
    )
    big, rest = add_up(gm.reshape(96, 16, 384), small.reshape(32, 16, 384))
    scale = (2.0 * 128000) ** (-0.5)
    rest = rest.reshape(512, 384)
    scaled = lambda a: a.astype(F32) * scale
    return (
        relayed[None],
        token_grad[None],
        scaled(rest[384, :C]),
        scaled(rest[192:384, :C]),
        scaled(rest[:192]),
        scaled(rest[192:384, C:]),
        scaled(big.reshape(1536, 384)),
    )


def solution(mesh):
    rows = P("stream", ("depth", "height"), None)
    cells = P("stream", "depth", "height", None)
    return jax.shard_map(
        local,
        mesh=mesh,
        in_specs=(cells, P(), P(), P(), P(), P(), P("depth", "height"), rows),
        out_specs=(rows, cells, P(), P(), P(), P(), P()),
        check_vma=False,
    )
```

time: 834 us -> 165 us (0.20); the launches traced: 825 us -> 165 us
  local copies, waits for them, and re-layouts: 352 us -> 0 us
  waiting for transfers between devices: 201 us -> 0 us
  Pallas kernels: 0 us -> 156 us
  blocking collectives: 88.6 us -> 0 us
  other arithmetic: 64.9 us -> 7.52 us
  matrix products: 55.1 us -> 0 us
  starting transfers between devices: 47.5 us -> 0 us
  between operations: 15.9 us -> 1.31 us
    psum x1 -> x0, waiting for transfers between devices: 166 us -> none  [local(): lax.psum((gain_part, query_wgrad, keyval_wgrad, out_wgrad, merge_wgrad),...]
    pallas_call x0 -> x5, Pallas kernels: none -> 156 us  [the longest x1 44.3 us: add_up(): pl.pallas_call(add_up_kernel, out_shape=(jax.ShapeDtypeStruct((96, 16, 38...]
    pad x4 -> x0, local copies, waits for them, and re-layouts: 145 us -> none  [the longest x2 72.6 us: window_rims(): after_rim = leading[6:number * 5 + 2:5][:, None]]
    psum x1 -> x0, blocking collectives: 88.6 us -> none  [local(): lax.psum((gain_part, query_wgrad, keyval_wgrad, out_wgrad, merge_wgrad),...]
    dot_general x21 -> x0, matrix products: 55.1 us -> none  [the longest x1 12.6 us: attend_backward(): jnp.einsum('nhqk,nqhd->nkhd', score_grad, query_heads, preferred_element_...]
    ppermute x16 -> x0, starting transfers between devices: 47.5 us -> none  [the longest x6 22.1 us: passed_along(): return lax.ppermute(block, axis, route)]
    ppermute x16 -> x0, waiting for transfers between devices: 35.4 us -> none  [the longest x6 29.5 us: passed_along(): return lax.ppermute(block, axis, route)]
    convert_element_type x16 -> x0, local copies, waits for them, and re-layouts: 32.2 us -> none  [the longest x5 15.2 us: local(): query_grad = window_grid(query_grad_w, depth_count, height_count, width_c...]
  transfers between devices with their start and end apart: 17 -> 0, of which waited for: 7 -> 0; matrix products, arithmetic and copies ran while one was open for 10% -> 0% of each run, Pallas kernels for 0% -> 0%
where the time goes in v1:
time: 165 us
  Pallas kernels  156 us (95%)
  other arithmetic  7.52 us (5%)
    pallas_call x1, Pallas kernels, add_up(): pl.pallas_call(add_up_kernel, out_shape=(jax.ShapeDtypeStruct((96, 16, 38...  44.3 us
    pallas_call x1, Pallas kernels, compute(): pl.pallas_call(compute_kernel, out_shape=(jax.ShapeDtypeStruct((128, 384)...  37.7 us
    pallas_call x1, Pallas kernels, intake(): pl.pallas_call(intake_kernel, out_shape=(jax.ShapeDtypeStruct((10, 16, 19...  34.1 us
    pallas_call x1, Pallas kernels, exchange(): pl.pallas_call(exchange_kernel, out_shape=(jax.ShapeDtypeStruct((10, 10,...  29.4 us
    pallas_call x1, Pallas kernels, finish(): pl.pallas_call(finish_kernel, out_shape=(jax.ShapeDtypeStruct((10, 10, 19...  10.2 us
    mul x4, other arithmetic, local(): scaled = lambda a: a.astype(F32) * scale  7.52 us

profile of v1, /device:TPU:1, one launch (start us, length us, event | category | flops | bytes accessed | tf_op | source)
XLA Modules:
  0.0 164.5 jit_solution(11504735854923008269)
XLA Ops:
  1.3 34.1 %intake.1 = (bf16[10,16,1920]{2,1,0:T(8,128)(2,1)}, bf16[12,16,1920]{2,1,0:T(8,128)(2,1)}, bf16[2,16,1920]{2,1,0:T(8,128)(2,1)}, bf16[4,16,1920]{2,1,0:T(8,128)(...) custom-call(bf16[10,10,1920]{2,1,0:T(8,128)(2,1)} %bitcast.13, bf16[3,48000]{1,0:T(4,128)(2,1)} %bitcast.15, ...), custom_call_target="tpu_custom_call" | custom-call | tf_op jit(solution)/shard_map/intake/pallas_call | solution.py:179
  35.4 37.7 %compute.1 = (bf16[128,384]{1,0:T(8,128)(2,1)}, bf16[1536,384]{1,0:T(8,128)(2,1)}, f32[192,192]{1,0:T(8,128)}, f32[10,10,16,192]{3,2,1,0:T(8,128)}, f32[10,10,16...) custom-call(bf16[10,16,1920]{2,1,0:T(8,128)(2,1)} %get-tuple-element, ...), custom_call_target="tpu_custom_call" | custom-call | tf_op jit(solution)/shard_map/compute/pallas_call | solution.py:394
  73.1 29.4 %exchange.1 = (bf16[10,10,16,384]{3,2,1,0:T(8,128)(2,1)}, bf16[2,10,16,384]{3,2,1,0:T(8,128)(2,1)}, bf16[2,10,16,384]{3,2,1,0:T(8,128)(2,1)}, bf16[4,16,384]{2,1,0:T(8,128)(2,1)}, bf16[2,128,384]{2,1,0:T(8,128)(2,1)}) custom-call(bf16[10,10,16,384]{3,2,1,0:T(8,128)(2,1)} %get-tuple-element.39.main, bf16[2,10,16,384]{3,2,1,0:T(8,128)(2,1)} %get-tuple-element.40.kd, ...), custom_call_target="tpu_custom_call" | custom-call | tf_op jit(solution)/shard_map/exchange/pallas_call | solution.py:461
  102.5 10.2 %finish.1 = (bf16[10,10,1920]{2,1,0:T(8,128)(2,1)}, bf16[3,48000]{1,0:T(4,128)(2,1)}, bf16[512,384]{1,0:T(8,128)(2,1)}) custom-call(bf16[10,16,1920]{2,1,0:T(8,128)(2,1)} %get-tuple-element.32.own_tok, f32[10,10,16,192]{3,2,1,0:T(8,128)} %get-tuple-element.37.qg, f32[10,10,16,192]{3,2,1,0:T(8,128)} %get-tuple-element.38.og, ...), custom_call_target="tpu_custom_call" | custom-call | tf_op jit(solution)/shard_map/finish/pallas_call | solution.py:571
  112.7 44.3 %add_up.1 = (bf16[96,16,384]{2,1,0:T(8,128)(2,1)}, bf16[32,16,384]{2,1,0:T(8,128)(2,1)}) custom-call(bf16[96,16,384]{2,1,0:T(8,128)(2,1)} %bitcast.12, bf16[32,16,384]{2,1,0:T(8,128)(2,1)} %bitcast.14), custom_call_target="tpu_custom_call" | custom-call | tf_op jit(solution)/shard_map/add_up/pallas_call | solution.py:709
  157.0 1.2 fusion
  158.3 1.6 %convert_multiply_fusion.1 = f32[12,16,384]{2,1,0:T(8,128)} fusion(bf16[32,16,384]{2,1,0:T(8,128)(2,1)} %get-tuple-element.55), kind=kLoop, calls=%fused_computation.1 | loop fusion | flops 147456 | bytes 442368 | tf_op jit(solution)/shard_map/mul | solution.py:758
  159.9 1.7 %convert_multiply_fusion.2 = (f32[192,192]{1,0:T(8,128)}, f32[192,192]{1,0:T(8,128)}) fusion(bf16[512,384]{1,0:T(8,128)(2,1)} %bitcast.17), kind=kLoop, calls=%fused_computation.2 | loop fusion | flops 147456 | bytes 442368 | tf_op jit(solution)/shard_map/mul | solution.py:758
  161.7 2.9 %convert_multiply_fusion = f32[96,16,384]{2,1,0:T(8,128)} fusion(bf16[96,16,384]{2,1,0:T(8,128)(2,1)} %get-tuple-element.56), kind=kLoop, calls=%fused_computation | loop fusion | flops 1179648 | bytes 3538944 | tf_op jit(solution)/shard_map/mul | solution.py:758

commit v2 on v0

v2 whole, which is shorter than its diff:
```python
import functools

import jax
import jax.numpy as jnp
import numpy as np
from jax import lax
from jax.experimental import pallas as pl
from jax.experimental.pallas import tpu as pltpu
from jax.sharding import PartitionSpec as P

C = 192
HEADS = 6
EPS = 1e-05
N_DEPTH = 4
N_HEIGHT = 32
SCALE = 32 ** (-0.5)
EXP2_SCALE = SCALE * 1.4426950408889634
MESH = pl.DeviceIdType.MESH
F32 = jnp.float32
BF16 = jnp.bfloat16
VM = pl.BlockSpec(memory_space=pltpu.VMEM)
SM = pl.BlockSpec(memory_space=pltpu.SMEM)
LIMIT = 60 * 1024 * 1024


def dot(a, b):
    return lax.dot_general(a, b, (((1,), (0,)), ((), ())), preferred_element_type=F32)


def dot_nt(a, b):
    return lax.dot_general(a, b, (((1,), (1,)), ((), ())), preferred_element_type=F32)


def dot_tn(a, b):
    return lax.dot_general(a, b, (((0,), (0,)), ((), ())), preferred_element_type=F32)


def place():
    return lax.axis_index("stream"), lax.axis_index("depth"), lax.axis_index("height")


def neighbours():
    s, d, h = place()
    dl, dh = lax.rem(d + N_DEPTH - 1, N_DEPTH), lax.rem(d + 1, N_DEPTH)
    hl, hh = lax.rem(h + N_HEIGHT - 1, N_HEIGHT), lax.rem(h + 1, N_HEIGHT)
    o = 1 - s
    return {
        "p": (o, d, h),
        "dl": (o, dl, h),
        "dh": (o, dh, h),
        "hl": (o, d, hl),
        "hh": (o, d, hh),
        "ll": (o, dl, hl),
        "lh": (o, dl, hh),
        "hdl": (o, dh, hl),
        "hdh": (o, dh, hh),
        "sl": (s, d, hl),
        "sh": (s, d, hh),
    }


def greet(peers):
    barrier = pltpu.get_barrier_semaphore()
    for peer in peers:
        pl.semaphore_signal(barrier, inc=1, device_id=peer, device_id_type=MESH)
    pl.semaphore_wait(barrier, len(peers))


def copier(send_sem, recv_sem):
    def make(src, dst, index, peer):
        return pltpu.make_async_remote_copy(
            src_ref=src,
            dst_ref=dst,
            send_sem=send_sem.at[index],
            recv_sem=recv_sem.at[index],
            device_id=peer,
            device_id_type=MESH,
        )

    return make


def relay_ranks(fl, fs, fr):
    _, _, h = place()
    left, right = lax.rem(h + N_HEIGHT - 1, N_HEIGHT), lax.rem(h + 1, N_HEIGHT)

    def before(a, b):
        return jnp.where(a < b, 1, 0)

    rank_l = fs * before(h, left) + fr * before(right, left)
    rank_s = fl * before(left, h) + fr * before(right, h)
    rank_r = fl * before(left, right) + fs * before(h, right)
    return rank_l, rank_s, rank_r


def wide(row):
    return jnp.concatenate([row, row, row], axis=1)


def normalized(x):
    centre = jnp.mean(x, -1, keepdims=True)
    shifted = x - centre
    inverse = lax.rsqrt(jnp.mean(shifted * shifted, -1, keepdims=True) + EPS)
    return shifted * inverse, inverse


def eight_index(window, q):
    wi, di, hi = window // 4, (window // 2) % 2, window % 2
    a = (q * 41) >> 10
    rest = q - a * 25
    b = (rest * 205) >> 10
    c = rest - b * 5
    w, d, h = a + 5 * wi, b + 5 * di, c + 5 * hi
    offset = ((d & 1) * 2 + (h & 1)) * 2 + (w & 1)
    cell = ((d >> 1) * 5 + (h >> 1)) * 5 + (w >> 1)
    return jnp.where(q < 125, offset * 128 + cell, -1)


def lane_row(tile):
    return jnp.concatenate([tile[j : j + 1] for j in range(15)], axis=1)


class Adder:
    def __init__(self, refs, send_sem, recv_sem):
        (self.src, self.out, self.r1, self.acc, self.snd2, self.r2a, self.r2b, self.acc2,
         self.snd3, self.r3a, self.r3b, self.r4, self.res4, self.res3, self.res2) = refs
        self.copy = copier(send_sem, recv_sem)
        s, d, h = place()
        zh, xy = h // 16, lax.rem(h, 16)
        x, y = xy // 4, lax.rem(xy, 4)
        self.s, self.x, self.y, self.z = s, x, y, zh * 4 + d
        self.partner = (1 - s, d, h)
        self.xk = [lax.rem(x + k, 4) for k in (1, 2, 3)]
        self.yk = [lax.rem(y + k, 4) for k in (1, 2, 3)]
        self.xs = [(s, d, zh * 16 + t * 4 + y) for t in self.xk]
        self.ys = [(s, d, zh * 16 + x * 4 + t) for t in self.yk]
        zk = [lax.rem(self.z + k, 8) for k in range(1, 8)]
        self.zk = zk
        self.zs = [(s, lax.rem(t, 4), (t // 4) * 16 + xy) for t in zk]

    def copies(self, step):
        c, x, y, z = self.copy, self.x, self.y, self.z
        three = range(3)
        if step == 1:
            return [c(self.src.at[1 - self.s], self.r1, 0, self.partner)]
        if step == 2:
            return [
                c(self.snd2.at[pl.ds(8 * self.xk[k], 8)], self.r2a.at[k], 1 + k, self.xs[k])
                for k in three
            ] + [
                c(self.snd2.at[pl.ds(32 + 4 * self.yk[k], 4)], self.r2b.at[k], 4 + k, self.ys[k])
                for k in three
            ]
        if step == 3:
            return [
                c(self.snd3.at[pl.ds(2 * self.yk[k], 2)], self.r3a.at[k], 7 + k, self.ys[k])
                for k in three
            ] + [
                c(self.snd3.at[8 + self.xk[k]], self.r3b.at[k], 10 + k, self.xs[k])
                for k in three
            ]
        if step == 4:
            return [c(self.r4.at[z], self.r4.at[z], 13 + k, self.zs[k]) for k in range(7)]
        if step == 5:
            return [
                c(self.res4.at[pl.ds(0, 2)], self.res3.at[pl.ds(2 * y, 2)], 20 + k, self.ys[k])
                for k in three
            ] + [c(self.res4.at[2], self.res3.at[8 + x], 23 + k, self.xs[k]) for k in three]
        if step == 6:
            return [
                c(self.res3.at[pl.ds(0, 8)], self.res2.at[pl.ds(8 * x, 8)], 26 + k, self.xs[k])
                for k in three
            ] + [
                c(self.res3.at[pl.ds(8, 4)], self.res2.at[pl.ds(32 + 4 * y, 4)], 29 + k, self.ys[k])
                for k in three
            ]
        return [c(self.res2, self.out.at[self.s], 32, self.partner)]

    def start(self, step):
        for one in self.copies(step):
            one.start()

    def finish(self, step):
        for one in self.copies(step):
            one.wait()
        x, y, z = self.x, self.y, self.z

        def total(first, parts):
            for part in parts:
                first = first + part.astype(F32)
            return first

        if step == 1:
            self.acc[...] = self.src[self.s].astype(F32) + self.r1[...].astype(F32)
            self.snd2[...] = self.acc[...].astype(BF16)
        elif step == 2:
            ra, rb = self.r2a, self.r2b
            self.acc2[0:8] = total(self.acc[pl.ds(8 * x, 8)], [ra[0], ra[1], ra[2]])
            self.acc2[8:12] = total(self.acc[pl.ds(32 + 4 * y, 4)], [rb[0], rb[1], rb[2]])
            self.snd3[...] = self.acc2[...].astype(BF16)
        elif step == 3:
            ra, rb = self.r3a, self.r3b
            self.r4[z, 0:2] = total(self.acc2[pl.ds(2 * y, 2)], [ra[0], ra[1], ra[2]]).astype(BF16)
            self.r4[z, 2] = total(self.acc2[8 + x], [rb[0], rb[1], rb[2]]).astype(BF16)
        elif step == 4:
            done = total(self.r4[0].astype(F32), [self.r4[k] for k in range(1, 8)]).astype(BF16)
            self.res4[...] = done
            self.res3[pl.ds(2 * y, 2)] = done[0:2]
            self.res3[8 + x] = done[2]
        elif step == 5:
            self.res2[pl.ds(8 * x, 8)] = self.res3[0:8]
            self.res2[pl.ds(32 + 4 * y, 4)] = self.res3[8:12]
        elif step == 6:
            self.out[self.s] = self.res2[...]

    def advance(self, step):
        self.finish(step)
        self.start(step + 1)


def adder_scratch(lanes, with_src):
    def of(*dims, kind=BF16):
        return pltpu.VMEM((*dims, 16, lanes), kind)

    return [of(2, 48)] * with_src + [
        of(48),
        of(48, kind=F32),
        of(48),
        of(3, 8),
        of(3, 4),
        of(12, kind=F32),
        of(12),
        of(3, 2),
        of(3),
        of(8, 3),
        of(3),
        of(12),
        of(48),
    ]


N_ADDER = 13


def whole_kernel(
    tok, rg, own, gain, wq, wkv, wo, wm, g, gt,
    token_grad, relayed, out_g, out_s,
    *scratch,
):
    (stage, own_tok, region, hstage, hsend, rims, cst, csend, corners, rimst, rimx,
     rows, mg_send, mg_recv, mg, own_send, owners,
     qreg, xreg, kreg, vreg, nreg, norm_n, inv_n, acck, accv, wk, wv,
     abuf, cts, qs, og_e, out_w, pt, qbd, qbd_t, cgbd, cgbd_t, ctx_t, qg_t, go, og_n,
     merged, r_merged, kv_h, r_h, kv_c, cstage, r_c, kv_main, r_main, kv_d, r_d,
     normals, kvs, qgs, stage2, wins, wide_out,
     send_sem, recv_sem, g_send, g_recv, s_send, s_recv) = scratch[:65]
    rest = scratch[65:]
    qg_n = qreg
    big = Adder((rest[0], out_g, *rest[1 : 1 + N_ADDER]), g_send, g_recv)
    rest = rest[1 + N_ADDER :]
    small = Adder((rest[0], out_s, *rest[1 : 1 + N_ADDER]), s_send, s_recv)
    s, dep, hei = place()
    peers = neighbours()
    copy = copier(send_sem, recv_sem)
    greeted = list(peers.values()) + big.xs + big.ys + big.zs
    barrier = pltpu.get_barrier_semaphore()
    for peer in greeted:
        pl.semaphore_signal(barrier, inc=1, device_id=peer, device_id_type=MESH)

    own_send[...] = jnp.full((8, 128), own[0, 0], jnp.int32)
    owners[1] = own_send[...]
    stage[...] = jnp.zeros_like(stage)
    hstage[...] = jnp.zeros_like(hstage)
    cst[...] = jnp.zeros_like(cst)
    for d in range(10):
        x = tok[d].astype(F32)
        stage[d, 1:7, :] = x[0:6]
        stage[d, 9:14, :] = x[5:10]
        stage[d, 8:9, :] = x[4:5]
        hstage[0, d : d + 1, :] = x[0:1]
        hstage[1, d : d + 1, :] = x[9:10]
        if d in (0, 9):
            for side in range(2):
                r = x[9 * side : 9 * side + 1]
                for j in range(15):
                    cst[2 * (d // 9) + side, j : j + 1, :] = r[:, 128 * j : 128 * j + 128]
    own_tok[...] = stage[...].astype(BF16)
    hsend[...] = hstage[...].astype(BF16)
    csend[...] = cst[...].astype(BF16)

    gains = gain[...]
    for pair in range(5):
        lanes = slice(384 * pair, 384 * pair + 384)
        own2 = stage[:, :, lanes].reshape(160, 384)
        for half in range(2):
            w = 2 * pair + half
            x = own2[:, 192 * half : 192 * half + 192]
            normed, inverse = normalized(x)
            norm_n[w] = normed
            inv_n[w] = inverse
            qreg[w] = dot((normed * gains).astype(BF16), wq[...]).reshape(10, 16, C)
            xreg[w] = x.reshape(10, 16, C)
    pl.semaphore_wait(barrier, len(greeted))
    to_left = copy(own_send, owners.at[2], 0, peers["sl"])
    to_right = copy(own_send, owners.at[0], 1, peers["sh"])
    far = [
        copy(hsend.at[1], rims.at[0], 5, peers["hh"]),
        copy(hsend.at[0], rims.at[1], 6, peers["hl"]),
        copy(csend.at[3], corners.at[0], 7, peers["hdh"]),
        copy(csend.at[2], corners.at[1], 8, peers["hdl"]),
        copy(csend.at[1], corners.at[2], 9, peers["lh"]),
        copy(csend.at[0], corners.at[3], 10, peers["ll"]),
    ]
    near = [
        copy(own_tok, region.at[pl.ds(1, 10)], 2, peers["p"]),
        copy(own_tok.at[9], region.at[0], 3, peers["dh"]),
        copy(own_tok.at[0], region.at[11], 4, peers["dl"]),
    ]
    to_left.start()
    to_right.start()
    for one in far + near:
        one.start()

    rows[...] = jnp.zeros_like(rows)

    def spread(i, carry):
        x = rg[:, pl.ds(pl.multiple_of(i * 384, 128), 384)].astype(F32)
        for k in range(3):
            rows[k, pl.ds(i, 1), :] = x[k : k + 1]
        return carry

    lax.fori_loop(0, 125, spread, 0)
    acck[...] = jnp.zeros_like(acck)
    accv[...] = jnp.zeros_like(accv)
    qbd_t[...] = jnp.zeros_like(qbd_t)
    cgbd_t[...] = jnp.zeros_like(cgbd_t)
    ones = lax.broadcasted_iota(jnp.int32, (64, 768), 0)
    qbd_t[192:256, :] = jnp.where(ones == 0, 1.0, 0.0).astype(BF16)
    go[...] = jnp.zeros_like(go)
    wk[...] = jnp.zeros_like(wk)
    wk[:, :C] = wkv[:, :C]
    wv[...] = wkv[:, C:]

    row = lax.broadcasted_iota(jnp.int32, (192, 256), 0)
    lane = lax.broadcasted_iota(jnp.int32, (192, 256), 1)
    rd, rs = row >> 4, row & 15
    off_depth = ((rd == 0) & (dep == 0)) | ((rd == 11) & (dep == N_DEPTH - 1))
    bias = jnp.where((off_depth | ((rs & 7) == 7)) & (lane == 192), -1e30, 0.0)
    edge = jnp.where(lane == 192, -1e30, 0.0).reshape(12, 16, 256)
    for w in (0, 11):
        kreg[w] = edge
        vreg[w] = jnp.zeros((12, 16, C), F32)

    for one in near:
        one.wait()
    for pair in range(5):
        lanes = slice(384 * pair, 384 * pair + 384)
        reg2 = region[:, :, lanes].astype(F32).reshape(192, 384)
        for half in range(2):
            w = 2 * pair + half
            y = reg2[:, 192 * half : 192 * half + 192]
            normed, _ = normalized(y)
            normal = (normed * gains).astype(BF16)
            nreg[w] = normed.reshape(12, 16, C)
            kreg[w + 1] = (dot(normal, wk[...]) + bias).reshape(12, 16, 256)
            vreg[w + 1] = dot(normal, wv[...]).reshape(12, 16, C)
    for one in far:
        one.wait()
    rimst[...] = jnp.zeros_like(rimst)
    for side in range(2):
        rimst[side, 1:11, :] = rims[side].astype(F32)[0:10]
        rimst[side, 0:1, :] = lane_row(corners[side].astype(F32))
        rimst[side, 11:12, :] = lane_row(corners[2 + side].astype(F32))
        for pair in range(5):
            x = rimst[side, :, 384 * pair : 384 * pair + 384]
            rimx[side, 2 * pair] = x[:, :C]
            rimx[side, 2 * pair + 1] = x[:, C:]
    rlane = lax.broadcasted_iota(jnp.int32, (160, 256), 1)
    rrow = lax.broadcasted_iota(jnp.int32, (160, 256), 0) & 15
    off_depth = ((rrow == 0) & (dep == 0)) | ((rrow == 11) & (dep == N_DEPTH - 1))
    for side in range(2):
        off = off_depth | (hei == (N_HEIGHT - 1) * side)
        rbias = jnp.where(off & (rlane == 192), -1e30, 0.0)
        normed, _ = normalized(rimx[side].reshape(160, C))
        normal = (normed * gains).astype(BF16)
        kr = (dot(normal, wk[...]) + rbias).reshape(10, 16, 256)
        vr = dot(normal, wv[...]).reshape(10, 16, C)
        nr = normed.reshape(10, 16, C)
        at = slice(14 * side, 14 * side + 1)
        for w in range(10):
            for d in range(12):
                kreg[w + 1, d, at, :] = kr[w, d : d + 1]
                vreg[w + 1, d, at, :] = vr[w, d : d + 1]
                nreg[w, d, at, :] = nr[w, d : d + 1]

    to_left.wait()
    to_right.wait()
    fl = jnp.where(owners[0, 0:1, :] == hei, 1, 0)
    fs = jnp.where(owners[1, 0:1, :] == hei, 1, 0)
    fr = jnp.where(owners[2, 0:1, :] == hei, 1, 0)
    rank_l, rank_s, rank_r = relay_ranks(fl, fs, fr)

    def pick_row(rank):
        rank = wide(rank)
        return jnp.where(rank == 0, rows[0], jnp.where(rank == 1, rows[1], rows[2]))

    mg_send[0] = pick_row(rank_l).astype(BF16)
    mg_send[1] = pick_row(rank_r).astype(BF16)
    back = [
        copy(mg_send.at[0], mg_recv.at[1], 11, peers["sl"]),
        copy(mg_send.at[1], mg_recv.at[0], 12, peers["sh"]),
    ]
    for one in back:
        one.start()

    def window_of(i, first):
        hi = (i // 4 + first) % 2
        di, wi = i % 2, (i // 2) % 2
        hs = pl.ds(pl.multiple_of(hi * 8, 8), 8)
        cells = (pl.ds(wi * 5, 5), pl.ds(di * 5, 5), hs, slice(None))
        around = (pl.ds(wi * 5, 7), pl.ds(di * 5, 7), hs, slice(None))
        return wi * 4 + di * 2 + hi, cells, around

    head = lax.broadcasted_iota(jnp.int32, (128, C), 1) >> 5
    odd = hei % 2

    def forward(i, carry):
        n, cells, around = window_of(i, 1 - odd)
        q_w = dot(gt[...], qreg[cells].reshape(200, C).astype(BF16))
        x_w = dot(gt[...], xreg[cells].reshape(200, C).astype(BF16))
        q = lax.broadcasted_iota(jnp.int32, (1024, 128), 1)
        col = lax.broadcasted_iota(jnp.int32, (1024, 128), 0)
        pt[n] = jnp.where(eight_index(n, q) == col, 1.0, 0.0).astype(BF16)
        qs[n] = q_w.astype(BF16)
        q_t = q_w.T.astype(BF16)
        for m in range(HEADS):
            r, l = slice(32 * m, 32 * m + 32), slice(128 * m, 128 * m + 128)
            qbd_t[r, l] = q_t[r]
        k = kreg[around].reshape(392, 256).astype(BF16)
        v_t = vreg[around].reshape(392, C).T.astype(BF16)
        for p in range(3):
            l = slice(256 * p, 256 * p + 256)
            e = jnp.exp2(dot(k, qbd_t[:, l]) * EXP2_SCALE)
            a = (e * (1.0 / jnp.sum(e, 0, keepdims=True))).astype(BF16)
            abuf[n, :, l] = a
            c = dot(v_t[64 * p : 64 * p + 64], a)
            ctx_t[64 * p : 64 * p + 32, :] = c[:32, :128]
            ctx_t[64 * p + 32 : 64 * p + 64, :] = c[32:, 128:]
        c_t = ctx_t[...]
        cts[n] = c_t.astype(BF16)
        out_w[n] = (dot(c_t.T.astype(BF16), wo[...]) + x_w).astype(BF16)
        return carry

    lax.fori_loop(0, 8, forward, 0)
    out_e = dot(pt[0], out_w[0])
    for i in range(1, 8):
        out_e = out_e + dot(pt[i], out_w[i])
    out_b = out_e.astype(BF16)
    total = jnp.zeros((128, 384), F32)
    for o in range(8):
        total = total + dot(out_b[128 * o : 128 * o + 128], wm[192 * o : 192 * o + 192, :])
    merged[...] = total.astype(BF16)
    relays = [
        copy(merged, r_merged.at[1], 13, peers["sl"]),
        copy(merged, r_merged.at[0], 14, peers["sh"]),
    ]
    for one in relays:
        one.start()
    left, right = lax.rem(hei + N_HEIGHT - 1, N_HEIGHT), lax.rem(hei + 1, N_HEIGHT)
    target = wide(owners[1, 0:1, :])
    mine = pick_row(rank_s)
    for one in back:
        one.wait()
    mg[...] = jnp.where(
        target == left,
        mg_recv[0].astype(F32),
        jnp.where(target == right, mg_recv[1].astype(F32), mine),
    ).astype(BF16)
    for o in range(8):
        part = dot_tn(out_b[128 * o : 128 * o + 128], mg[...]).astype(BF16)
        big.src[o // 4, 12 * (o % 4) : 12 * (o % 4) + 12] = part.reshape(12, 16, 384)
    big.start(1)
    for o in range(8):
        og_e[128 * o : 128 * o + 128, :] = dot_nt(
            mg[...], wm[192 * o : 192 * o + 192, :]
        ).astype(BF16)

    cstage[...] = jnp.zeros_like(cstage)
    srow = lax.broadcasted_iota(jnp.int32, (16, 192), 0)
    scol = lax.broadcasted_iota(jnp.int32, (16, 192), 1)

    def rim_copies(side):
        hn = lax.rem(hei + 2 * side + N_HEIGHT - 1, N_HEIGHT)
        dl, dh = lax.rem(dep + N_DEPTH - 1, N_DEPTH), lax.rem(dep + 1, N_DEPTH)
        return [
            copy(kv_h.at[side], r_h.at[1 - side], 15 + side, (1 - s, dep, hn)),
            copy(kv_c.at[side], r_c.at[3 - side], 17 + side, (1 - s, dl, hn)),
            copy(kv_c.at[2 + side], r_c.at[1 - side], 19 + side, (1 - s, dh, hn)),
        ]

    def send_rim(side):
        pick = jnp.where(scol == srow * 16 + 14 * side, 1.0, 0.0).astype(BF16)
        for w in range(10):
            t = jnp.concatenate([acck[w + 1], accv[w + 1]], axis=-1)
            r = dot(pick, t.reshape(192, 384).astype(BF16))
            kv_h[side, w] = r.astype(BF16)
            cstage[0, w : w + 1, :] = r[0:1]
            cstage[1, w : w + 1, :] = r[11:12]
        kv_c[side] = cstage[0].astype(BF16)
        kv_c[2 + side] = cstage[1].astype(BF16)
        for one in rim_copies(side):
            one.start()

    def backward(i, carry):
        n, cells, around = window_of(i, odd)
        q = lax.broadcasted_iota(jnp.int32, (128, 1024), 0)
        col = lax.broadcasted_iota(jnp.int32, (128, 1024), 1)
        pick = jnp.where(eight_index(n, q) == col, 1.0, 0.0).astype(BF16)
        og_b = dot(pick, og_e[...]).astype(BF16)
        cg_w = dot_nt(og_b, wo[...]).astype(BF16).astype(F32)
        q_w = qs[n].astype(F32)
        cg_t = cg_w.T.astype(BF16)
        for m in range(HEADS):
            r, l = slice(32 * m, 32 * m + 32), slice(128 * m, 128 * m + 128)
            cgbd_t[r, l] = cg_t[r]
            qbd[l, :] = jnp.where(head == m, q_w, 0.0).astype(BF16)
            cgbd[l, :] = jnp.where(head == m, cg_w, 0.0).astype(BF16)
        k_t = kreg[around].reshape(392, 256)[:, :C].T.astype(BF16)
        v = vreg[around].reshape(392, C).astype(BF16)
        kg = jnp.zeros((392, C), F32)
        vg = jnp.zeros((392, C), F32)
        for p in range(3):
            l = slice(256 * p, 256 * p + 256)
            a = abuf[n, :, l]
            af = a.astype(F32)
            wg = dot(v, cgbd_t[:, l])
            mean = jnp.sum(wg * af, 0, keepdims=True)
            sg = (af * (wg - mean) * SCALE).astype(BF16)
            vg = vg + dot(a, cgbd[l, :])
            kg = kg + dot(sg, qbd[l, :])
            c = dot(k_t[64 * p : 64 * p + 64], sg)
            qg_t[64 * p : 64 * p + 32, :] = c[:32, :128]
            qg_t[64 * p + 32 : 64 * p + 64, :] = c[32:, 128:]
        acck[around] += kg.reshape(7, 7, 8, C)
        accv[around] += vg.reshape(7, 7, 8, C)
        go[...] += dot(cts[n], og_b)
        qg_w = qg_t[...].T.astype(BF16)
        qg_n[cells] = dot(g[...], qg_w).reshape(5, 5, 8, C)
        og_n[cells] = dot(g[...], og_b).reshape(5, 5, 8, C)
        for at, step in ((0, 1), (1, 2), (2, 3), (4, 4), (5, 5), (6, 6)):
            pl.when(i == at)(functools.partial(big.advance, step))
        pl.when(i == 3)(functools.partial(send_rim, odd))
        return carry

    lax.fori_loop(0, 8, backward, 0)

    send_rim(1 - odd)
    slot = lax.broadcasted_iota(jnp.int32, (12, 16, 384), 1)
    inner = (slot & 7 >= 1) & (slot & 7 <= 5)
    for w in range(10):
        t = jnp.concatenate([acck[w + 1], accv[w + 1]], axis=-1)
        kvs[192 * w : 192 * w + 192, :] = t.reshape(192, 384).astype(BF16)
        t = t + jnp.where(slot == 5, t[:, 8:9, :], jnp.where(slot == 9, t[:, 6:7, :], 0.0))
        b = jnp.where(inner, t, 0.0).astype(BF16)
        kv_main[w] = b[1:11]
        kv_d[0, w] = b[0]
        kv_d[1, w] = b[11]
    grads = [
        copy(kv_d.at[0], r_d.at[1], 21, peers["dl"]),
        copy(kv_d.at[1], r_d.at[0], 22, peers["dh"]),
        copy(kv_main, r_main, 23, peers["p"]),
    ]
    for one in grads:
        one.start()

    gain_sum = jnp.zeros((1, C), F32)
    for w in range(10):
        normed = nreg[w].reshape(192, C)
        normals[192 * w : 192 * w + 192, :] = (normed * gains).astype(BF16)
        ng = dot_nt(kvs[192 * w : 192 * w + 192, :], wkv[...])
        gain_sum = gain_sum + jnp.sum(ng * normed, 0, keepdims=True)
    part = dot_tn(normals[...], kvs[...]).astype(BF16)
    for j in range(3):
        small.src[0, 12 * j : 12 * j + 12] = part[:, 128 * j : 128 * j + 128].reshape(12, 16, 128)
    for w in range(10):
        normed = norm_n[w]
        normals[160 * w : 160 * w + 160, :] = (normed * gains).astype(BF16)
        qgs[160 * w : 160 * w + 160, :] = qg_n[w].reshape(160, C).astype(BF16)
        ng = dot_nt(qgs[160 * w : 160 * w + 160, :], wq[...])
        xreg[w] = ng.reshape(10, 16, C)
        gain_sum = gain_sum + jnp.sum(ng * normed, 0, keepdims=True)
    part = jnp.concatenate([dot_tn(normals[0:1600, :], qgs[...]), go[...]], axis=1).astype(BF16)
    for j in range(3):
        small.src[1, 12 * j : 12 * j + 12] = part[:, 128 * j : 128 * j + 128].reshape(12, 16, 128)
    first = lax.broadcasted_iota(jnp.int32, (16, 128), 0)
    tail = jnp.concatenate([gain_sum[:, 128:], jnp.zeros((1, 64), F32)], axis=1)
    small.src[:, 36:48] = jnp.zeros((2, 12, 16, 128), BF16)
    small.src[0, 36] = jnp.where(
        first == 0, gain_sum[:, :128], jnp.where(first == 1, tail, 0.0)
    ).astype(BF16)
    small.start(1)

    for one in relays:
        one.wait()
    parts = []
    for flag, rank, win in zip(
        (fl, fs, fr), (rank_l, rank_s, rank_r), (r_merged[0], merged[...], r_merged[1])
    ):
        parts.append((wide(jnp.where(flag == 1, rank, -1)), win.astype(F32)))
    for k in range(3):
        total = jnp.zeros((128, 384), F32)
        for key, win in parts:
            total = jnp.where(key == k, win, total)
        wins[k] = total
    small.advance(1)

    def lay(i, carry):
        lanes = pl.ds(pl.multiple_of(i * 384, 128), 384)
        for k in range(3):
            wide_out[k : k + 1, lanes] = wins[k, pl.ds(i, 1), :]
        return carry

    lax.fori_loop(0, 125, lay, 0)
    relayed[...] = wide_out[...].astype(BF16)
    small.advance(2)
    for one in grads + rim_copies(0) + rim_copies(1):
        one.wait()

    sl = lax.broadcasted_iota(jnp.int32, (16, 384), 0)
    for pair in range(5):
        lanes = slice(384 * pair, 384 * pair + 384)
        found = []
        for half in range(2):
            w = 2 * pair + half
            lo, hi = r_h[0, w].astype(F32), r_h[1, w].astype(F32)
            planes = []
            for d in range(10):
                lo_d, hi_d = lo[d + 1 : d + 2], hi[d + 1 : d + 2]
                if d in (0, 9):
                    e = 2 * (d // 9)
                    lo_d = lo_d + r_c[e].astype(F32)[w : w + 1]
                    hi_d = hi_d + r_c[e + 1].astype(F32)[w : w + 1]
                t = r_main[w, d].astype(F32)
                t = t + jnp.where(sl == 1, lo_d, jnp.where(sl == 13, hi_d, 0.0))
                if d in (0, 9):
                    t = t + r_d[d // 9, w].astype(F32)
                planes.append(t.astype(BF16))
            kv_b = jnp.concatenate(planes, axis=0)
            normed, inverse = norm_n[w], inv_n[w]
            u = (xreg[w].reshape(160, C) + dot_nt(kv_b, wkv[...])) * gains
            found.append(
                inverse
                * (
                    u
                    - jnp.mean(u, -1, keepdims=True)
                    - normed * jnp.mean(u * normed, -1, keepdims=True)
                )
                + og_n[w].reshape(160, C)
            )
        stage[:, :, lanes] = jnp.concatenate(found, axis=1).reshape(10, 16, 384)
        if pair in (0, 1, 3, 4):
            small.advance({0: 3, 1: 4, 3: 5, 4: 6}[pair])
    for d in range(10):
        x = stage[d]
        stage2[d, 0:5, :] = x[1:6]
        stage2[d, 5:10, :] = x[9:14]
    token_grad[...] = stage2[...].astype(BF16)
    small.finish(7)
    big.finish(7)


def whole(tok, rg, own, gain, wq, wkv, wo, wm):
    g = np.zeros((200, 128), np.float32)
    for a in range(5):
        for b in range(5):
            for c in range(5):
                g[(a * 5 + b) * 8 + c + 1, a * 25 + b * 5 + c] = 1
    g = jnp.asarray(g, BF16)
    vm, dma = pltpu.VMEM, pltpu.SemaphoreType.DMA
    scratch = [
        vm((10, 16, 1920), F32),
        vm((10, 16, 1920), BF16),
        vm((12, 16, 1920), BF16),
        vm((2, 16, 1920), F32),
        vm((2, 16, 1920), BF16),
        vm((2, 16, 1920), BF16),
        vm((4, 16, 128), F32),
        vm((4, 16, 128), BF16),
        vm((4, 16, 128), BF16),
        vm((2, 16, 1920), F32),
        vm((2, 10, 16, C), F32),
        vm((3, 128, 384), F32),
        vm((2, 128, 384), BF16),
        vm((2, 128, 384), BF16),
        vm((128, 384), BF16),
        vm((8, 128), jnp.int32),
        vm((3, 8, 128), jnp.int32),
        vm((10, 10, 16, C), F32),
        vm((10, 10, 16, C), F32),
        vm((12, 12, 16, 256), F32),
        vm((12, 12, 16, C), F32),
        vm((10, 12, 16, C), F32),
        vm((10, 160, C), F32),
        vm((10, 160, 1), F32),
        vm((12, 12, 16, C), F32),
        vm((12, 12, 16, C), F32),
        vm((C, 256), BF16),
        vm((C, C), BF16),
        vm((8, 392, 768), BF16),
        vm((8, C, 128), BF16),
        vm((8, 128, C), BF16),
        vm((1024, C), BF16),
        vm((8, 128, C), BF16),
        vm((8, 1024, 128), BF16),
        vm((768, C), BF16),
        vm((256, 768), BF16),
        vm((768, C), BF16),
        vm((C, 768), BF16),
        vm((C, 128), F32),
        vm((C, 128), F32),
        vm((C, C), F32),
        vm((10, 10, 16, C), F32),
        vm((128, 384), BF16),
        vm((2, 128, 384), BF16),
        vm((2, 10, 16, 384), BF16),
        vm((2, 10, 16, 384), BF16),
        vm((4, 16, 384), BF16),
        vm((2, 16, 384), F32),
        vm((4, 16, 384), BF16),
        vm((10, 10, 16, 384), BF16),
        vm((10, 10, 16, 384), BF16),
        vm((2, 10, 16, 384), BF16),
        vm((2, 10, 16, 384), BF16),
        vm((1920, C), BF16),
        vm((1920, 384), BF16),
        vm((1600, C), BF16),
        vm((10, 10, 1920), F32),
        vm((3, 128, 384), F32),
        vm((3, 48000), F32),
        dma((24,)), dma((24,)),
        dma((33,)), dma((33,)),
        dma((33,)), dma((33,)),
    ]
    scratch += adder_scratch(384, True) + adder_scratch(128, True)
    return pl.pallas_call(
        whole_kernel,
        out_shape=(
            jax.ShapeDtypeStruct((10, 10, 1920), BF16),
            jax.ShapeDtypeStruct((3, 48000), BF16),
            jax.ShapeDtypeStruct((2, 48, 16, 384), BF16),
            jax.ShapeDtypeStruct((2, 48, 16, 128), BF16),
        ),
        in_specs=[VM, VM, SM] + [VM] * 7,
        out_specs=(VM,) * 4,
        scratch_shapes=scratch,
        compiler_params=pltpu.CompilerParams(
            collective_id=1, has_side_effects=True, vmem_limit_bytes=LIMIT
        ),
        name="whole",
    )(tok, rg, own, gain, wq, wkv, wo, wm, g, g.T)


def local(tokens, ln_gain, w_query, w_keyval, w_out, w_merge, owner_map, relay_grad):
    token_grad, relayed, big, small = whole(
        tokens[0], relay_grad[0], owner_map, ln_gain.reshape(1, C), w_query, w_keyval, w_out,
        w_merge,
    )
    scale = (2.0 * 128000) ** (-0.5)
    scaled = lambda a: a.astype(F32) * scale

    def joined(half):
        tiles = small[half, :36].reshape(3, 12 * 16, 128)
        return jnp.concatenate([tiles[0], tiles[1], tiles[2]], axis=1)

    keyval, both = joined(0), joined(1)
    return (
        relayed[None],
        token_grad[None],
        scaled(small[0, 36, 0:2].reshape(256)[:C]),
        scaled(both[:, :C]),
        scaled(keyval),
        scaled(both[:, C:]),
        scaled(big.reshape(1536, 384)),
    )

def solution(mesh):
    rows = P("stream", ("depth", "height"), None)
    cells = P("stream", "depth", "height", None)
    return jax.shard_map(
        local,
        mesh=mesh,
        in_specs=(cells, P(), P(), P(), P(), P(), P("depth", "height"), rows),
        out_specs=(rows, cells, P(), P(), P(), P(), P()),
        check_vma=False,
    )
```

time: 834 us -> 119 us (0.14); the launches traced: 825 us -> 119 us
  local copies, waits for them, and re-layouts: 352 us -> 3.29 us
  waiting for transfers between devices: 201 us -> 0 us
  Pallas kernels: 0 us -> 111 us
  blocking collectives: 88.6 us -> 0 us
  other arithmetic: 64.9 us -> 3.71 us
  matrix products: 55.1 us -> 0 us
  starting transfers between devices: 47.5 us -> 0 us
  between operations: 15.9 us -> 1.31 us
    psum x1 -> x0, waiting for transfers between devices: 166 us -> none  [local(): lax.psum((gain_part, query_wgrad, keyval_wgrad, out_wgrad, merge_wgrad),...]
    pad x4 -> x0, local copies, waits for them, and re-layouts: 145 us -> none  [the longest x2 72.6 us: window_rims(): after_rim = leading[6:number * 5 + 2:5][:, None]]
    pallas_call x0 -> x1, Pallas kernels: none -> 111 us  [whole(): pl.pallas_call(whole_kernel, out_shape=(jax.ShapeDtypeStruct((10, 10, 192...]
    psum x1 -> x0, blocking collectives: 88.6 us -> none  [local(): lax.psum((gain_part, query_wgrad, keyval_wgrad, out_wgrad, merge_wgrad),...]
    dot_general x21 -> x0, matrix products: 55.1 us -> none  [the longest x1 12.6 us: attend_backward(): jnp.einsum('nhqk,nqhd->nkhd', score_grad, query_heads, preferred_element_...]
    ppermute x16 -> x0, starting transfers between devices: 47.5 us -> none  [the longest x6 22.1 us: passed_along(): return lax.ppermute(block, axis, route)]
    ppermute x16 -> x0, waiting for transfers between devices: 35.4 us -> none  [the longest x6 29.5 us: passed_along(): return lax.ppermute(block, axis, route)]
    convert_element_type x16 -> x0, local copies, waits for them, and re-layouts: 32.2 us -> none  [the longest x5 15.2 us: local(): query_grad = window_grid(query_grad_w, depth_count, height_count, width_c...]
  transfers between devices with their start and end apart: 17 -> 0, of which waited for: 7 -> 0; matrix products, arithmetic and copies ran while one was open for 10% -> 0% of each run, Pallas kernels for 0% -> 0%
where the time goes in v2:
time: 119 us
  Pallas kernels  111 us (93%)
  other arithmetic  3.71 us (3%)
  local copies, waits for them, and re-layouts  3.29 us (3%)
  between operations  1.31 us (1%)
    pallas_call x1, Pallas kernels, whole(): pl.pallas_call(whole_kernel, out_shape=(jax.ShapeDtypeStruct((10, 10, 192...  111 us
    mul x4, other arithmetic, local(): scaled = lambda a: a.astype(F32) * scale  3.71 us

profile of v2, /device:TPU:1, one launch (start us, length us, event | category | flops | bytes accessed | tf_op | source)
XLA Modules:
  0.0 119.2 jit_solution(9809978975590533174)
XLA Ops:
  1.3 110.9 %whole.1 = (bf16[10,10,1920]{2,1,0:T(8,128)(2,1)}, bf16[3,48000]{1,0:T(4,128)(2,1)}, bf16[2,48,16,384]{3,2,1,0:T(8,128)(2,1)}, bf16[2,48,16,128]{3,2,1,0:T(8,128)(2,1)}) custom-call(bf16[10,10,1920]{2,1,0:T(8,128)(2,1)} %bitcast.15, bf16[3,48000]{1,0:T(4,128)(2,1)} %bitcast.17, s32[1,1]{1,0:T(1,128)S(6)} %copy.18.own, f32[1,192]{1,0:T(1,128)} %bitcast.25, ...), custom_call_target="tpu_custom_call" | custom-call | tf_op jit(solution)/shard_map/whole/pallas_call | solution.py:745
  112.2 0.0 copy-start
  112.2 0.8 slice_bitcast_fusion
  112.9 0.9 fusion
  113.9 0.0 copy-start.2
  113.9 0.6 convert_multiply_fusion.4
  114.5 0.7 convert_multiply_fusion.1
  115.2 0.0 copy-start.1
  115.2 0.8 convert_multiply_fusion.2
  116.0 0.0 copy-done
  116.0 1.6 %convert_multiply_fusion = f32[2,48,16,384]{3,2,1,0:T(8,128)} fusion(bf16[2,48,16,384]{3,2,1,0:T(8,128)(2,1)S(1)} %copy-done), kind=kLoop, calls=%fused_computation | loop fusion | flops 1179648 | bytes 3538944 | tf_op jit(solution)/shard_map/mul | solution.py:769
  117.6 0.0 copy-done.2
  117.6 0.7 copy.19
  118.4 0.0 copy-done.1
  118.4 0.8 copy.20
Async XLA Ops:
  112.2 3.8 %copy-start = (bf16[2,48,16,384]{3,2,1,0:T(8,128)(2,1)S(1)}, bf16[2,48,16,384]{3,2,1,0:T(8,128)(2,1)}, u32[]{:S(2)}) copy-start(bf16[2,48,16,384]{3,2,1,0:T(8,128)(2,1)} %get-tuple-element.14) | copy-start | bytes 3538948
  113.9 3.7 %copy-start.2 = (bf16[3,48000]{1,0:T(4,128)(2,1)S(1)}, bf16[3,48000]{1,0:T(4,128)(2,1)}, u32[]{:S(2)}) copy-start(bf16[3,48000]{1,0:T(4,128)(2,1)} %get-tuple-element.11) | copy-start | bytes 864004
  115.2 3.2 %copy-start.1 = (bf16[10,10,1920]{2,1,0:T(8,128)(2,1)S(1)}, bf16[10,10,1920]{2,1,0:T(8,128)(2,1)}, u32[]{:S(2)}) copy-start(bf16[10,10,1920]{2,1,0:T(8,128)(2,1)} %get-tuple-element.12) | copy-start | bytes 1152004

commit v3 on v2

--- a/solution.py
+++ b/solution.py
@@ -20,7 +20,7 @@
 BF16 = jnp.bfloat16
 VM = pl.BlockSpec(memory_space=pltpu.VMEM)
 SM = pl.BlockSpec(memory_space=pltpu.SMEM)
-LIMIT = 60 * 1024 * 1024
+LIMIT = 62 * 1024 * 1024
 
 
 def dot(a, b):
@@ -122,59 +122,35 @@
 
 class Adder:
     def __init__(self, refs, send_sem, recv_sem):
-        (self.src, self.out, self.r1, self.acc, self.snd2, self.r2a, self.r2b, self.acc2,
-         self.snd3, self.r3a, self.r3b, self.r4, self.res4, self.res3, self.res2) = refs
+        (self.src, self.out, self.r1, self.snd2, self.r2, self.r4, self.res4,
+         self.res2) = refs
         self.copy = copier(send_sem, recv_sem)
         s, d, h = place()
         zh, xy = h // 16, lax.rem(h, 16)
-        x, y = xy // 4, lax.rem(xy, 4)
-        self.s, self.x, self.y, self.z = s, x, y, zh * 4 + d
+        self.s, self.xy, self.z = s, xy, zh * 4 + d
         self.partner = (1 - s, d, h)
-        self.xk = [lax.rem(x + k, 4) for k in (1, 2, 3)]
-        self.yk = [lax.rem(y + k, 4) for k in (1, 2, 3)]
-        self.xs = [(s, d, zh * 16 + t * 4 + y) for t in self.xk]
-        self.ys = [(s, d, zh * 16 + x * 4 + t) for t in self.yk]
-        zk = [lax.rem(self.z + k, 8) for k in range(1, 8)]
-        self.zk = zk
-        self.zs = [(s, lax.rem(t, 4), (t // 4) * 16 + xy) for t in zk]
+        self.pk = [lax.rem(xy + k, 16) for k in range(1, 16)]
+        self.ps = [(s, d, zh * 16 + t) for t in self.pk]
+        self.zs = []
+        for k in range(1, 8):
+            t = lax.rem(self.z + k, 8)
+            self.zs.append((s, lax.rem(t, 4), (t // 4) * 16 + xy))
 
     def copies(self, step):
-        c, x, y, z = self.copy, self.x, self.y, self.z
-        three = range(3)
+        c, xy, z = self.copy, self.xy, self.z
         if step == 1:
             return [c(self.src.at[1 - self.s], self.r1, 0, self.partner)]
         if step == 2:
             return [
-                c(self.snd2.at[pl.ds(8 * self.xk[k], 8)], self.r2a.at[k], 1 + k, self.xs[k])
-                for k in three
-            ] + [
-                c(self.snd2.at[pl.ds(32 + 4 * self.yk[k], 4)], self.r2b.at[k], 4 + k, self.ys[k])
-                for k in three
+                c(self.snd2.at[pl.ds(3 * self.pk[k], 3)], self.r2.at[k], 1 + k, self.ps[k])
+                for k in range(15)
             ]
         if step == 3:
-            return [
-                c(self.snd3.at[pl.ds(2 * self.yk[k], 2)], self.r3a.at[k], 7 + k, self.ys[k])
-                for k in three
-            ] + [
-                c(self.snd3.at[8 + self.xk[k]], self.r3b.at[k], 10 + k, self.xs[k])
-                for k in three
-            ]
+            return [c(self.r4.at[z], self.r4.at[z], 16 + k, self.zs[k]) for k in range(7)]
         if step == 4:
-            return [c(self.r4.at[z], self.r4.at[z], 13 + k, self.zs[k]) for k in range(7)]
-        if step == 5:
-            return [
-                c(self.res4.at[pl.ds(0, 2)], self.res3.at[pl.ds(2 * y, 2)], 20 + k, self.ys[k])
-                for k in three
-            ] + [c(self.res4.at[2], self.res3.at[8 + x], 23 + k, self.xs[k]) for k in three]
-        if step == 6:
-            return [
-                c(self.res3.at[pl.ds(0, 8)], self.res2.at[pl.ds(8 * x, 8)], 26 + k, self.xs[k])
-                for k in three
-            ] + [
-                c(self.res3.at[pl.ds(8, 4)], self.res2.at[pl.ds(32 + 4 * y, 4)], 29 + k, self.ys[k])
-                for k in three
-            ]
-        return [c(self.res2, self.out.at[self.s], 32, self.partner)]
+            at = pl.ds(3 * xy, 3)
+            return [c(self.res4, self.res2.at[at], 23 + k, self.ps[k]) for k in range(15)]
+        return [c(self.res2, self.out.at[self.s], 38, self.partner)]
 
     def start(self, step):
         for one in self.copies(step):
@@ -183,34 +159,24 @@
     def finish(self, step):
         for one in self.copies(step):
             one.wait()
-        x, y, z = self.x, self.y, self.z
-
-        def total(first, parts):
-            for part in parts:
-                first = first + part.astype(F32)
-            return first
-
+        xy, z = self.xy, self.z
         if step == 1:
-            self.acc[...] = self.src[self.s].astype(F32) + self.r1[...].astype(F32)
-            self.snd2[...] = self.acc[...].astype(BF16)
+            total = self.src[self.s].astype(F32) + self.r1[...].astype(F32)
+            self.snd2[...] = total.astype(BF16)
         elif step == 2:
-            ra, rb = self.r2a, self.r2b
-            self.acc2[0:8] = total(self.acc[pl.ds(8 * x, 8)], [ra[0], ra[1], ra[2]])
-            self.acc2[8:12] = total(self.acc[pl.ds(32 + 4 * y, 4)], [rb[0], rb[1], rb[2]])
-            self.snd3[...] = self.acc2[...].astype(BF16)
+            at = pl.ds(3 * xy, 3)
+            total = self.src[self.s, at].astype(F32) + self.r1[at].astype(F32)
+            for k in range(15):
+                total = total + self.r2[k].astype(F32)
+            self.r4[z] = total.astype(BF16)
         elif step == 3:
-            ra, rb = self.r3a, self.r3b
-            self.r4[z, 0:2] = total(self.acc2[pl.ds(2 * y, 2)], [ra[0], ra[1], ra[2]]).astype(BF16)
-            self.r4[z, 2] = total(self.acc2[8 + x], [rb[0], rb[1], rb[2]]).astype(BF16)
+            total = self.r4[0].astype(F32)
+            for k in range(1, 8):
+                total = total + self.r4[k].astype(F32)
+            done = total.astype(BF16)
+            self.res4[...] = done
+            self.res2[pl.ds(3 * xy, 3)] = done
         elif step == 4:
-            done = total(self.r4[0].astype(F32), [self.r4[k] for k in range(1, 8)]).astype(BF16)
-            self.res4[...] = done
-            self.res3[pl.ds(2 * y, 2)] = done[0:2]
-            self.res3[8 + x] = done[2]
-        elif step == 5:
-            self.res2[pl.ds(8 * x, 8)] = self.res3[0:8]
-            self.res2[pl.ds(32 + 4 * y, 4)] = self.res3[8:12]
-        elif step == 6:
             self.out[self.s] = self.res2[...]
 
     def advance(self, step):
@@ -218,28 +184,14 @@
         self.start(step + 1)
 
 
-def adder_scratch(lanes, with_src):
-    def of(*dims, kind=BF16):
-        return pltpu.VMEM((*dims, 16, lanes), kind)
-
-    return [of(2, 48)] * with_src + [
-        of(48),
-        of(48, kind=F32),
-        of(48),
-        of(3, 8),
-        of(3, 4),
-        of(12, kind=F32),
-        of(12),
-        of(3, 2),
-        of(3),
-        of(8, 3),
-        of(3),
-        of(12),
-        of(48),
-    ]
-
-
-N_ADDER = 13
+def adder_scratch(lanes):
+    def of(*dims):
+        return pltpu.VMEM((*dims, 16, lanes), BF16)
+
+    return [of(2, 48), of(48), of(48), of(15, 3), of(8, 3), of(3), of(48)]
+
+
+N_ADDER = 6
 
 
 def whole_kernel(
@@ -250,11 +202,11 @@
     (stage, own_tok, region, hstage, hsend, rims, cst, csend, corners, rimst, rimx,
      rows, mg_send, mg_recv, mg, own_send, owners,
      qreg, xreg, kreg, vreg, nreg, norm_n, inv_n, acck, accv, wk, wv,
-     abuf, cts, qs, og_e, out_w, pt, qbd, qbd_t, cgbd, cgbd_t, ctx_t, qg_t, go, og_n,
+     abuf, cts, qs, og_e, out_b, out_w, pt, pw, sgs, qbd, qbd_t, cgbd, cgbd_t, ctx_t, qg_t, go, og_n,
      merged, r_merged, kv_h, r_h, kv_c, cstage, r_c, kv_main, r_main, kv_d, r_d,
      normals, kvs, qgs, stage2, wins, wide_out,
-     send_sem, recv_sem, g_send, g_recv, s_send, s_recv) = scratch[:65]
-    rest = scratch[65:]
+     send_sem, recv_sem, g_send, g_recv, s_send, s_recv) = scratch[:68]
+    rest = scratch[68:]
     qg_n = qreg
     big = Adder((rest[0], out_g, *rest[1 : 1 + N_ADDER]), g_send, g_recv)
     rest = rest[1 + N_ADDER :]
@@ -262,7 +214,7 @@
     s, dep, hei = place()
     peers = neighbours()
     copy = copier(send_sem, recv_sem)
-    greeted = list(peers.values()) + big.xs + big.ys + big.zs
+    greeted = list(peers.values()) + big.ps + big.zs
     barrier = pltpu.get_barrier_semaphore()
     for peer in greeted:
         pl.semaphore_signal(barrier, inc=1, device_id=peer, device_id_type=MESH)
@@ -288,18 +240,39 @@
     hsend[...] = hstage[...].astype(BF16)
     csend[...] = cst[...].astype(BF16)
 
-    gains = gain[...]
-    for pair in range(5):
-        lanes = slice(384 * pair, 384 * pair + 384)
-        own2 = stage[:, :, lanes].reshape(160, 384)
-        for half in range(2):
-            w = 2 * pair + half
-            x = own2[:, 192 * half : 192 * half + 192]
-            normed, inverse = normalized(x)
-            norm_n[w] = normed
-            inv_n[w] = inverse
-            qreg[w] = dot((normed * gains).astype(BF16), wq[...]).reshape(10, 16, C)
-            xreg[w] = x.reshape(10, 16, C)
+    rows[...] = jnp.zeros_like(rows)
+
+    def spread(i, carry):
+        x = rg[:, pl.ds(pl.multiple_of(i * 384, 128), 384)].astype(F32)
+        for k in range(3):
+            rows[k, pl.ds(i, 1), :] = x[k : k + 1]
+        return carry
+
+    lax.fori_loop(0, 125, spread, 0)
+    acck[...] = jnp.zeros_like(acck)
+    accv[...] = jnp.zeros_like(accv)
+    qbd_t[...] = jnp.zeros_like(qbd_t)
+    cgbd_t[...] = jnp.zeros_like(cgbd_t)
+    ones = lax.broadcasted_iota(jnp.int32, (64, 768), 0)
+    qbd_t[192:256, :] = jnp.where(ones == 0, 1.0, 0.0).astype(BF16)
+    go[...] = jnp.zeros_like(go)
+    wk[...] = jnp.zeros_like(wk)
+    wk[:, :C] = wkv[:, :C]
+    wv[...] = wkv[:, C:]
+
+    def maps(n, carry):
+        index = eight_index(n, lax.broadcasted_iota(jnp.int32, (1, 128), 1))
+        col = lax.broadcasted_iota(jnp.int32, (1024, 128), 0)
+        at = pl.ds(pl.multiple_of(n * 128, 128), 128)
+        pt[:, at] = jnp.where(index == col, 1.0, 0.0).astype(BF16)
+        index = eight_index(n, lax.broadcasted_iota(jnp.int32, (128, 128), 0))
+        col = lax.broadcasted_iota(jnp.int32, (128, 128), 1)
+        for o in range(8):
+            hit = jnp.where(index == col + 128 * o, 1.0, 0.0).astype(BF16)
+            pw[n, :, 128 * o : 128 * o + 128] = hit
+        return carry
+
+    lax.fori_loop(0, 8, maps, 0)
     pl.semaphore_wait(barrier, len(greeted))
     to_left = copy(own_send, owners.at[2], 0, peers["sl"])
     to_right = copy(own_send, owners.at[0], 1, peers["sh"])
@@ -321,26 +294,18 @@
     for one in far + near:
         one.start()
 
-    rows[...] = jnp.zeros_like(rows)
-
-    def spread(i, carry):
-        x = rg[:, pl.ds(pl.multiple_of(i * 384, 128), 384)].astype(F32)
-        for k in range(3):
-            rows[k, pl.ds(i, 1), :] = x[k : k + 1]
-        return carry
-
-    lax.fori_loop(0, 125, spread, 0)
-    acck[...] = jnp.zeros_like(acck)
-    accv[...] = jnp.zeros_like(accv)
-    qbd_t[...] = jnp.zeros_like(qbd_t)
-    cgbd_t[...] = jnp.zeros_like(cgbd_t)
-    ones = lax.broadcasted_iota(jnp.int32, (64, 768), 0)
-    qbd_t[192:256, :] = jnp.where(ones == 0, 1.0, 0.0).astype(BF16)
-    go[...] = jnp.zeros_like(go)
-    wk[...] = jnp.zeros_like(wk)
-    wk[:, :C] = wkv[:, :C]
-    wv[...] = wkv[:, C:]
-
+    gains = gain[...]
+    for pair in range(5):
+        lanes = slice(384 * pair, 384 * pair + 384)
+        own2 = stage[:, :, lanes].reshape(160, 384)
+        for half in range(2):
+            w = 2 * pair + half
+            x = own2[:, 192 * half : 192 * half + 192]
+            normed, inverse = normalized(x)
+            norm_n[w] = normed
+            inv_n[w] = inverse
+            qreg[w] = dot((normed * gains).astype(BF16), wq[...]).reshape(10, 16, C)
+            xreg[w] = x.reshape(10, 16, C)
     row = lax.broadcasted_iota(jnp.int32, (192, 256), 0)
     lane = lax.broadcasted_iota(jnp.int32, (192, 256), 1)
     rd, rs = row >> 4, row & 15
@@ -364,6 +329,26 @@
             nreg[w] = normed.reshape(12, 16, C)
             kreg[w + 1] = (dot(normal, wk[...]) + bias).reshape(12, 16, 256)
             vreg[w + 1] = dot(normal, wv[...]).reshape(12, 16, C)
+    to_left.wait()
+    to_right.wait()
+    fl = jnp.where(owners[0, 0:1, :] == hei, 1, 0)
+    fs = jnp.where(owners[1, 0:1, :] == hei, 1, 0)
+    fr = jnp.where(owners[2, 0:1, :] == hei, 1, 0)
+    rank_l, rank_s, rank_r = relay_ranks(fl, fs, fr)
+
+    def pick_row(rank):
+        rank = wide(rank)
+        return jnp.where(rank == 0, rows[0], jnp.where(rank == 1, rows[1], rows[2]))
+
+    mg_send[0] = pick_row(rank_l).astype(BF16)
+    mg_send[1] = pick_row(rank_r).astype(BF16)
+    back = [
+        copy(mg_send.at[0], mg_recv.at[1], 11, peers["sl"]),
+        copy(mg_send.at[1], mg_recv.at[0], 12, peers["sh"]),
+    ]
+    for one in back:
+        one.start()
+
     for one in far:
         one.wait()
     rimst[...] = jnp.zeros_like(rimst)
@@ -393,26 +378,6 @@
                 vreg[w + 1, d, at, :] = vr[w, d : d + 1]
                 nreg[w, d, at, :] = nr[w, d : d + 1]
 
-    to_left.wait()
-    to_right.wait()
-    fl = jnp.where(owners[0, 0:1, :] == hei, 1, 0)
-    fs = jnp.where(owners[1, 0:1, :] == hei, 1, 0)
-    fr = jnp.where(owners[2, 0:1, :] == hei, 1, 0)
-    rank_l, rank_s, rank_r = relay_ranks(fl, fs, fr)
-
-    def pick_row(rank):
-        rank = wide(rank)
-        return jnp.where(rank == 0, rows[0], jnp.where(rank == 1, rows[1], rows[2]))
-
-    mg_send[0] = pick_row(rank_l).astype(BF16)
-    mg_send[1] = pick_row(rank_r).astype(BF16)
-    back = [
-        copy(mg_send.at[0], mg_recv.at[1], 11, peers["sl"]),
-        copy(mg_send.at[1], mg_recv.at[0], 12, peers["sh"]),
-    ]
-    for one in back:
-        one.start()
-
     def window_of(i, first):
         hi = (i // 4 + first) % 2
         di, wi = i % 2, (i // 2) % 2
@@ -428,9 +393,6 @@
         n, cells, around = window_of(i, 1 - odd)
         q_w = dot(gt[...], qreg[cells].reshape(200, C).astype(BF16))
         x_w = dot(gt[...], xreg[cells].reshape(200, C).astype(BF16))
-        q = lax.broadcasted_iota(jnp.int32, (1024, 128), 1)
-        col = lax.broadcasted_iota(jnp.int32, (1024, 128), 0)
-        pt[n] = jnp.where(eight_index(n, q) == col, 1.0, 0.0).astype(BF16)
         qs[n] = q_w.astype(BF16)
         q_t = q_w.T.astype(BF16)
         for m in range(HEADS):
@@ -448,17 +410,16 @@
             ctx_t[64 * p + 32 : 64 * p + 64, :] = c[32:, 128:]
         c_t = ctx_t[...]
         cts[n] = c_t.astype(BF16)
-        out_w[n] = (dot(c_t.T.astype(BF16), wo[...]) + x_w).astype(BF16)
+        at = pl.ds(pl.multiple_of(n * 128, 128), 128)
+        out_w[at, :] = (dot(c_t.T.astype(BF16), wo[...]) + x_w).astype(BF16)
         return carry
 
     lax.fori_loop(0, 8, forward, 0)
-    out_e = dot(pt[0], out_w[0])
-    for i in range(1, 8):
-        out_e = out_e + dot(pt[i], out_w[i])
-    out_b = out_e.astype(BF16)
     total = jnp.zeros((128, 384), F32)
     for o in range(8):
-        total = total + dot(out_b[128 * o : 128 * o + 128], wm[192 * o : 192 * o + 192, :])
+        part = dot(pt[128 * o : 128 * o + 128, :], out_w[...]).astype(BF16)
+        out_b[128 * o : 128 * o + 128, :] = part
+        total = total + dot(part, wm[192 * o : 192 * o + 192, :])
     merged[...] = total.astype(BF16)
     relays = [
         copy(merged, r_merged.at[1], 13, peers["sl"]),
@@ -477,14 +438,14 @@
         jnp.where(target == right, mg_recv[1].astype(F32), mine),
     ).astype(BF16)
     for o in range(8):
-        part = dot_tn(out_b[128 * o : 128 * o + 128], mg[...]).astype(BF16)
-        big.src[o // 4, 12 * (o % 4) : 12 * (o % 4) + 12] = part.reshape(12, 16, 384)
-    big.start(1)
-    for o in range(8):
         og_e[128 * o : 128 * o + 128, :] = dot_nt(
             mg[...], wm[192 * o : 192 * o + 192, :]
         ).astype(BF16)
 
+    for o in range(8):
+        part = dot_tn(out_b[128 * o : 128 * o + 128, :], mg[...]).astype(BF16)
+        big.src[o // 4, 12 * (o % 4) : 12 * (o % 4) + 12] = part.reshape(12, 16, 384)
+    big.start(1)
     cstage[...] = jnp.zeros_like(cstage)
     srow = lax.broadcasted_iota(jnp.int32, (16, 192), 0)
     scol = lax.broadcasted_iota(jnp.int32, (16, 192), 1)
@@ -513,10 +474,7 @@
 
     def backward(i, carry):
         n, cells, around = window_of(i, odd)
-        q = lax.broadcasted_iota(jnp.int32, (128, 1024), 0)
-        col = lax.broadcasted_iota(jnp.int32, (128, 1024), 1)
-        pick = jnp.where(eight_index(n, q) == col, 1.0, 0.0).astype(BF16)
-        og_b = dot(pick, og_e[...]).astype(BF16)
+        og_b = dot(pw[n], og_e[...]).astype(BF16)
         cg_w = dot_nt(og_b, wo[...]).astype(BF16).astype(F32)
         q_w = qs[n].astype(F32)
         cg_t = cg_w.T.astype(BF16)
@@ -527,8 +485,6 @@
             cgbd[l, :] = jnp.where(head == m, cg_w, 0.0).astype(BF16)
         k_t = kreg[around].reshape(392, 256)[:, :C].T.astype(BF16)
         v = vreg[around].reshape(392, C).astype(BF16)
-        kg = jnp.zeros((392, C), F32)
-        vg = jnp.zeros((392, C), F32)
         for p in range(3):
             l = slice(256 * p, 256 * p + 256)
             a = abuf[n, :, l]
@@ -536,18 +492,17 @@
             wg = dot(v, cgbd_t[:, l])
             mean = jnp.sum(wg * af, 0, keepdims=True)
             sg = (af * (wg - mean) * SCALE).astype(BF16)
-            vg = vg + dot(a, cgbd[l, :])
-            kg = kg + dot(sg, qbd[l, :])
+            sgs[:, l] = sg
             c = dot(k_t[64 * p : 64 * p + 64], sg)
             qg_t[64 * p : 64 * p + 32, :] = c[:32, :128]
             qg_t[64 * p + 32 : 64 * p + 64, :] = c[32:, 128:]
-        acck[around] += kg.reshape(7, 7, 8, C)
-        accv[around] += vg.reshape(7, 7, 8, C)
+        acck[around] += dot(sgs[...], qbd[...]).reshape(7, 7, 8, C)
+        accv[around] += dot(abuf[n], cgbd[...]).reshape(7, 7, 8, C)
         go[...] += dot(cts[n], og_b)
         qg_w = qg_t[...].T.astype(BF16)
         qg_n[cells] = dot(g[...], qg_w).reshape(5, 5, 8, C)
         og_n[cells] = dot(g[...], og_b).reshape(5, 5, 8, C)
-        for at, step in ((0, 1), (1, 2), (2, 3), (4, 4), (5, 5), (6, 6)):
+        for at, step in ((2, 1), (6, 2)):
             pl.when(i == at)(functools.partial(big.advance, step))
         pl.when(i == 3)(functools.partial(send_rim, odd))
         return carry
@@ -622,6 +577,7 @@
 
     lax.fori_loop(0, 125, lay, 0)
     relayed[...] = wide_out[...].astype(BF16)
+    big.advance(3)
     small.advance(2)
     for one in grads + rim_copies(0) + rim_copies(1):
         one.wait()
@@ -658,15 +614,17 @@
                 + og_n[w].reshape(160, C)
             )
         stage[:, :, lanes] = jnp.concatenate(found, axis=1).reshape(10, 16, 384)
-        if pair in (0, 1, 3, 4):
-            small.advance({0: 3, 1: 4, 3: 5, 4: 6}[pair])
+        if pair == 2:
+            big.advance(4)
+            small.advance(3)
+    small.advance(4)
     for d in range(10):
         x = stage[d]
         stage2[d, 0:5, :] = x[1:6]
         stage2[d, 5:10, :] = x[9:14]
     token_grad[...] = stage2[...].astype(BF16)
-    small.finish(7)
-    big.finish(7)
+    big.finish(5)
+    small.finish(5)
 
 
 def whole(tok, rg, own, gain, wq, wkv, wo, wm):
@@ -710,8 +668,11 @@
         vm((8, C, 128), BF16),
         vm((8, 128, C), BF16),
         vm((1024, C), BF16),
-        vm((8, 128, C), BF16),
-        vm((8, 1024, 128), BF16),
+        vm((1024, C), BF16),
+        vm((1024, C), BF16),
+        vm((1024, 1024), BF16),
+        vm((8, 128, 1024), BF16),
+        vm((392, 768), BF16),
         vm((768, C), BF16),
         vm((256, 768), BF16),
         vm((768, C), BF16),
@@ -738,10 +699,10 @@
         vm((3, 128, 384), F32),
         vm((3, 48000), F32),
         dma((24,)), dma((24,)),
-        dma((33,)), dma((33,)),
-        dma((33,)), dma((33,)),
+        dma((39,)), dma((39,)),
+        dma((39,)), dma((39,)),
     ]
-    scratch += adder_scratch(384, True) + adder_scratch(128, True)
+    scratch += adder_scratch(384) + adder_scratch(128)
     return pl.pallas_call(
         whole_kernel,
         out_shape=(
@@ -760,28 +721,55 @@
     )(tok, rg, own, gain, wq, wkv, wo, wm, g, g.T)
 
 
+def tail_kernel(
+    token_in, relayed_in, big, small, token_grad, relayed, gain, query, keyval, out, merge
+):
+    scale = (2.0 * 128000) ** (-0.5)
+    token_grad[...] = token_in[...]
+    relayed[...] = relayed_in[...]
+    merge[...] = (big[...].astype(F32) * scale).reshape(1536, 384)
+
+    def joined(half):
+        tiles = [
+            small[half, 12 * j : 12 * j + 12].astype(F32).reshape(192, 128) for j in range(3)
+        ]
+        return jnp.concatenate(tiles, axis=1) * scale
+
+    keyval[...] = joined(0)
+    both = joined(1)
+    query[...] = both[:, :C]
+    out[...] = both[:, C:]
+    sums = small[0, 36].astype(F32)
+    gain[...] = jnp.concatenate([sums[0:1], sums[1:2, : C - 128]], axis=1) * scale
+
+
+def tail(token_grad, relayed, big, small):
+    return pl.pallas_call(
+        tail_kernel,
+        out_shape=(
+            jax.ShapeDtypeStruct((10, 10, 1920), BF16),
+            jax.ShapeDtypeStruct((3, 48000), BF16),
+            jax.ShapeDtypeStruct((1, C), F32),
+            jax.ShapeDtypeStruct((C, C), F32),
+            jax.ShapeDtypeStruct((C, 384), F32),
+            jax.ShapeDtypeStruct((C, C), F32),
+            jax.ShapeDtypeStruct((1536, 384), F32),
+        ),
+        in_specs=[VM] * 4,
+        out_specs=(VM,) * 7,
+        compiler_params=pltpu.CompilerParams(vmem_limit_bytes=LIMIT),
+        name="tail",
+    )(token_grad, relayed, big, small)
+
+
 def local(tokens, ln_gain, w_query, w_keyval, w_out, w_merge, owner_map, relay_grad):
-    token_grad, relayed, big, small = whole(
+    results = whole(
         tokens[0], relay_grad[0], owner_map, ln_gain.reshape(1, C), w_query, w_keyval, w_out,
         w_merge,
     )
-    scale = (2.0 * 128000) ** (-0.5)
-    scaled = lambda a: a.astype(F32) * scale
-
-    def joined(half):
-        tiles = small[half, :36].reshape(3, 12 * 16, 128)
-        return jnp.concatenate([tiles[0], tiles[1], tiles[2]], axis=1)
-
-    keyval, both = joined(0), joined(1)
-    return (
-        relayed[None],
-        token_grad[None],
-        scaled(small[0, 36, 0:2].reshape(256)[:C]),
-        scaled(both[:, :C]),
-        scaled(keyval),
-        scaled(both[:, C:]),
-        scaled(big.reshape(1536, 384)),
-    )
+    token_grad, relayed, gain, query, keyval, out, merge = tail(*results)
+    return (relayed[None], token_grad[None], gain.reshape(C), query, keyval, out, merge)
+
 
 def solution(mesh):
     rows = P("stream", ("depth", "height"), None)

time: 119 us -> 92 us (0.77)
  Pallas kernels: 111 us -> 90.5 us
  other arithmetic: 3.71 us -> 0 us
  local copies, waits for them, and re-layouts: 3.29 us -> 0 us
    pallas_call x1, Pallas kernels: 111 us -> 86.8 us  [whole(): pl.pallas_call(whole_kernel, out_shape=(jax.ShapeDtypeStruct((10, 10, 192...]
    pallas_call x0 -> x1, Pallas kernels: none -> 3.71 us  [tail(): pl.pallas_call(tail_kernel, out_shape=(jax.ShapeDtypeStruct((10, 10, 1920...]
    mul x4 -> x0, other arithmetic: 3.71 us -> none  [local(): scaled = lambda a: a.astype(F32) * scale]
    unnamed x8 -> x0, local copies, waits for them, and re-layouts: 1.58 us -> none
where the time goes in v3:
time: 92 us; the launch traced here: 91.8 us
  Pallas kernels  90.5 us (98%)
  between operations  1.29 us (1%)
    pallas_call x1, Pallas kernels, whole(): pl.pallas_call(whole_kernel, out_shape=(jax.ShapeDtypeStruct((10, 10, 192...  86.8 us
    pallas_call x1, Pallas kernels, tail(): pl.pallas_call(tail_kernel, out_shape=(jax.ShapeDtypeStruct((10, 10, 1920...  3.71 us

profile of v3, /device:TPU:1, one launch (start us, length us, event | category | flops | bytes accessed | tf_op | source)
XLA Modules:
  0.0 91.8 jit_solution(1523064570032526230)
XLA Ops:
  1.3 86.8 %whole.1 = (bf16[10,10,1920]{2,1,0:T(8,128)(2,1)}, bf16[3,48000]{1,0:T(4,128)(2,1)}, bf16[2,48,16,384]{3,2,1,0:T(8,128)(2,1)}, bf16[2,48,16,128]{3,2,1,0:T(8,128)(2,1)}) custom-call(bf16[10,10,1920]{2,1,0:T(8,128)(2,1)} %bitcast.6, bf16[3,48000]{1,0:T(4,128)(2,1)} %bitcast.7, s32[1,1]{1,0:T(1,128)S(6)} %copy.16.own, f32[1,192]{1,0:T(1,128)} %bitcast.8, ...), custom_call_target="tpu_custom_call" | custom-call | tf_op jit(solution)/shard_map/whole/pallas_call | solution.py:706
  88.1 3.7 %tail.1 = (bf16[10,10,1920]{2,1,0:T(8,128)(2,1)}, bf16[3,48000]{1,0:T(4,128)(2,1)}, f32[1,192]{1,0:T(1,128)}, f32[192,192]{1,0:T(8,128)}, f32[192,384]{1,0:T(8,1...) custom-call(bf16[10,10,1920]{2,1,0:T(8,128)(2,1)} %get-tuple-element.18.token_in, ...), custom_call_target="tpu_custom_call" | custom-call | tf_op jit(solution)/shard_map/tail/pallas_call | solution.py:747

commit v4 on v3

--- a/solution.py
+++ b/solution.py
@@ -195,18 +195,18 @@
 
 
 def whole_kernel(
-    tok, rg, own, gain, wq, wkv, wo, wm, g, gt,
+    tok, rg, own, gain, wq, wkv, wo, wm_hbm, g, gt,
     token_grad, relayed, out_g, out_s,
     *scratch,
 ):
     (stage, own_tok, region, hstage, hsend, rims, cst, csend, corners, rimst, rimx,
      rows, mg_send, mg_recv, mg, own_send, owners,
      qreg, xreg, kreg, vreg, nreg, norm_n, inv_n, acck, accv, wk, wv,
-     abuf, cts, qs, og_e, out_b, out_w, pt, pw, sgs, qbd, qbd_t, cgbd, cgbd_t, ctx_t, qg_t, go, og_n,
+     abuf, cts, qs, og_e, out_b, og_all, cg_all, out_w, pt, pw, sgs, eye, wm, wm_sem, qbd, qbd_t, cgbd, cgbd_t, ctx_t, qg_t, og_n,
      merged, r_merged, kv_h, r_h, kv_c, cstage, r_c, kv_main, r_main, kv_d, r_d,
      normals, kvs, qgs, stage2, wins, wide_out,
-     send_sem, recv_sem, g_send, g_recv, s_send, s_recv) = scratch[:68]
-    rest = scratch[68:]
+     send_sem, recv_sem, g_send, g_recv, s_send, s_recv) = scratch[:72]
+    rest = scratch[72:]
     qg_n = qreg
     big = Adder((rest[0], out_g, *rest[1 : 1 + N_ADDER]), g_send, g_recv)
     rest = rest[1 + N_ADDER :]
@@ -215,6 +215,8 @@
     peers = neighbours()
     copy = copier(send_sem, recv_sem)
     greeted = list(peers.values()) + big.ps + big.zs
+    fetch = pltpu.make_async_copy(wm_hbm, wm, wm_sem)
+    fetch.start()
     barrier = pltpu.get_barrier_semaphore()
     for peer in greeted:
         pl.semaphore_signal(barrier, inc=1, device_id=peer, device_id_type=MESH)
@@ -248,14 +250,13 @@
             rows[k, pl.ds(i, 1), :] = x[k : k + 1]
         return carry
 
-    lax.fori_loop(0, 125, spread, 0)
+    lax.fori_loop(0, 125, spread, 0, unroll=5)
     acck[...] = jnp.zeros_like(acck)
     accv[...] = jnp.zeros_like(accv)
     qbd_t[...] = jnp.zeros_like(qbd_t)
     cgbd_t[...] = jnp.zeros_like(cgbd_t)
     ones = lax.broadcasted_iota(jnp.int32, (64, 768), 0)
     qbd_t[192:256, :] = jnp.where(ones == 0, 1.0, 0.0).astype(BF16)
-    go[...] = jnp.zeros_like(go)
     wk[...] = jnp.zeros_like(wk)
     wk[:, :C] = wkv[:, :C]
     wv[...] = wkv[:, C:]
@@ -269,10 +270,14 @@
         col = lax.broadcasted_iota(jnp.int32, (128, 128), 1)
         for o in range(8):
             hit = jnp.where(index == col + 128 * o, 1.0, 0.0).astype(BF16)
-            pw[n, :, 128 * o : 128 * o + 128] = hit
+            pw[at, 128 * o : 128 * o + 128] = hit
         return carry
 
     lax.fori_loop(0, 8, maps, 0)
+    diagonal = lax.broadcasted_iota(jnp.int32, (C, C), 0) == lax.broadcasted_iota(
+        jnp.int32, (C, C), 1
+    )
+    eye[...] = jnp.where(diagonal, 1.0, 0.0).astype(BF16)
     pl.semaphore_wait(barrier, len(greeted))
     to_left = copy(own_send, owners.at[2], 0, peers["sl"])
     to_right = copy(own_send, owners.at[0], 1, peers["sh"])
@@ -399,7 +404,7 @@
             r, l = slice(32 * m, 32 * m + 32), slice(128 * m, 128 * m + 128)
             qbd_t[r, l] = q_t[r]
         k = kreg[around].reshape(392, 256).astype(BF16)
-        v_t = vreg[around].reshape(392, C).T.astype(BF16)
+        v_t = dot_nt(eye[...], vreg[around].reshape(392, C).astype(BF16)).astype(BF16)
         for p in range(3):
             l = slice(256 * p, 256 * p + 256)
             e = jnp.exp2(dot(k, qbd_t[:, l]) * EXP2_SCALE)
@@ -409,12 +414,13 @@
             ctx_t[64 * p : 64 * p + 32, :] = c[:32, :128]
             ctx_t[64 * p + 32 : 64 * p + 64, :] = c[32:, 128:]
         c_t = ctx_t[...]
-        cts[n] = c_t.astype(BF16)
         at = pl.ds(pl.multiple_of(n * 128, 128), 128)
+        cts[:, at] = c_t.astype(BF16)
         out_w[at, :] = (dot(c_t.T.astype(BF16), wo[...]) + x_w).astype(BF16)
         return carry
 
-    lax.fori_loop(0, 8, forward, 0)
+    lax.fori_loop(0, 8, forward, 0, unroll=2)
+    fetch.wait()
     total = jnp.zeros((128, 384), F32)
     for o in range(8):
         part = dot(pt[128 * o : 128 * o + 128, :], out_w[...]).astype(BF16)
@@ -442,6 +448,8 @@
             mg[...], wm[192 * o : 192 * o + 192, :]
         ).astype(BF16)
 
+    og_all[...] = dot(pw[...], og_e[...]).astype(BF16)
+    cg_all[...] = dot_nt(og_all[...], wo[...]).astype(BF16)
     for o in range(8):
         part = dot_tn(out_b[128 * o : 128 * o + 128, :], mg[...]).astype(BF16)
         big.src[o // 4, 12 * (o % 4) : 12 * (o % 4) + 12] = part.reshape(12, 16, 384)
@@ -474,8 +482,9 @@
 
     def backward(i, carry):
         n, cells, around = window_of(i, odd)
-        og_b = dot(pw[n], og_e[...]).astype(BF16)
-        cg_w = dot_nt(og_b, wo[...]).astype(BF16).astype(F32)
+        at = pl.ds(pl.multiple_of(n * 128, 128), 128)
+        og_b = og_all[at, :]
+        cg_w = cg_all[at, :].astype(F32)
         q_w = qs[n].astype(F32)
         cg_t = cg_w.T.astype(BF16)
         for m in range(HEADS):
@@ -483,7 +492,7 @@
             cgbd_t[r, l] = cg_t[r]
             qbd[l, :] = jnp.where(head == m, q_w, 0.0).astype(BF16)
             cgbd[l, :] = jnp.where(head == m, cg_w, 0.0).astype(BF16)
-        k_t = kreg[around].reshape(392, 256)[:, :C].T.astype(BF16)
+        k_t = dot_nt(eye[...], kreg[around].reshape(392, 256)[:, :C].astype(BF16)).astype(BF16)
         v = vreg[around].reshape(392, C).astype(BF16)
         for p in range(3):
             l = slice(256 * p, 256 * p + 256)
@@ -498,7 +507,6 @@
             qg_t[64 * p + 32 : 64 * p + 64, :] = c[32:, 128:]
         acck[around] += dot(sgs[...], qbd[...]).reshape(7, 7, 8, C)
         accv[around] += dot(abuf[n], cgbd[...]).reshape(7, 7, 8, C)
-        go[...] += dot(cts[n], og_b)
         qg_w = qg_t[...].T.astype(BF16)
         qg_n[cells] = dot(g[...], qg_w).reshape(5, 5, 8, C)
         og_n[cells] = dot(g[...], og_b).reshape(5, 5, 8, C)
@@ -544,7 +552,7 @@
         ng = dot_nt(qgs[160 * w : 160 * w + 160, :], wq[...])
         xreg[w] = ng.reshape(10, 16, C)
         gain_sum = gain_sum + jnp.sum(ng * normed, 0, keepdims=True)
-    part = jnp.concatenate([dot_tn(normals[0:1600, :], qgs[...]), go[...]], axis=1).astype(BF16)
+    part = jnp.concatenate([dot_tn(normals[0:1600, :], qgs[...]), dot(cts[...], og_all[...])], axis=1).astype(BF16)
     for j in range(3):
         small.src[1, 12 * j : 12 * j + 12] = part[:, 128 * j : 128 * j + 128].reshape(12, 16, 128)
     first = lax.broadcasted_iota(jnp.int32, (16, 128), 0)
@@ -575,7 +583,7 @@
             wide_out[k : k + 1, lanes] = wins[k, pl.ds(i, 1), :]
         return carry
 
-    lax.fori_loop(0, 125, lay, 0)
+    lax.fori_loop(0, 125, lay, 0, unroll=5)
     relayed[...] = wide_out[...].astype(BF16)
     big.advance(3)
     small.advance(2)
@@ -665,21 +673,25 @@
         vm((C, 256), BF16),
         vm((C, C), BF16),
         vm((8, 392, 768), BF16),
-        vm((8, C, 128), BF16),
+        vm((C, 1024), BF16),
         vm((8, 128, C), BF16),
         vm((1024, C), BF16),
         vm((1024, C), BF16),
         vm((1024, C), BF16),
+        vm((1024, C), BF16),
+        vm((1024, C), BF16),
         vm((1024, 1024), BF16),
-        vm((8, 128, 1024), BF16),
+        vm((1024, 1024), BF16),
         vm((392, 768), BF16),
+        vm((C, C), BF16),
+        vm((1536, 384), BF16),
+        dma(()),
         vm((768, C), BF16),
         vm((256, 768), BF16),
         vm((768, C), BF16),
         vm((C, 768), BF16),
         vm((C, 128), F32),
         vm((C, 128), F32),
-        vm((C, C), F32),
         vm((10, 10, 16, C), F32),
         vm((128, 384), BF16),
         vm((2, 128, 384), BF16),
@@ -711,7 +723,7 @@
             jax.ShapeDtypeStruct((2, 48, 16, 384), BF16),
             jax.ShapeDtypeStruct((2, 48, 16, 128), BF16),
         ),
-        in_specs=[VM, VM, SM] + [VM] * 7,
+        in_specs=[VM, VM, SM] + [VM] * 4 + [pl.BlockSpec(memory_space=pl.ANY)] + [VM] * 2,
         out_specs=(VM,) * 4,
         scratch_shapes=scratch,
         compiler_params=pltpu.CompilerParams(

time: 92 us -> 90.9 us (0.988)
  Pallas kernels: 90.5 us -> 89.5 us
    pallas_call x1, Pallas kernels: 86.8 us -> 85.7 us  [whole(): pl.pallas_call(whole_kernel, out_shape=(jax.ShapeDtypeStruct((10, 10, 192...]
where the time goes in v4:
time: 90.9 us; the launch traced here: 90.8 us
  Pallas kernels  89.5 us (98%)
  between operations  1.29 us (1%)
    pallas_call x1, Pallas kernels, whole(): pl.pallas_call(whole_kernel, out_shape=(jax.ShapeDtypeStruct((10, 10, 192...  85.7 us
    pallas_call x1, Pallas kernels, tail(): pl.pallas_call(tail_kernel, out_shape=(jax.ShapeDtypeStruct((10, 10, 1920...  3.71 us

profile of v4, /device:TPU:1, one launch (start us, length us, event | category | flops | bytes accessed | tf_op | source)
XLA Modules:
  0.0 90.8 jit_solution(3343653901361281379)
XLA Ops:
  1.3 85.7 %whole.1 = (bf16[10,10,1920]{2,1,0:T(8,128)(2,1)}, bf16[3,48000]{1,0:T(4,128)(2,1)}, bf16[2,48,16,384]{3,2,1,0:T(8,128)(2,1)}, bf16[2,48,16,128]{3,2,1,0:T(8,128)(2,1)}) custom-call(bf16[10,10,1920]{2,1,0:T(8,128)(2,1)} %bitcast.6, bf16[3,48000]{1,0:T(4,128)(2,1)} %bitcast.7, s32[1,1]{1,0:T(1,128)S(6)} %copy.16.own, f32[1,192]{1,0:T(1,128)} %bitcast.8, ...), custom_call_target="tpu_custom_call" | custom-call | tf_op jit(solution)/shard_map/whole/pallas_call | solution.py:718
  87.0 3.7 %tail.1 = (bf16[10,10,1920]{2,1,0:T(8,128)(2,1)}, bf16[3,48000]{1,0:T(4,128)(2,1)}, f32[1,192]{1,0:T(1,128)}, f32[192,192]{1,0:T(8,128)}, f32[192,384]{1,0:T(8,1...) custom-call(bf16[10,10,1920]{2,1,0:T(8,128)(2,1)} %get-tuple-element.18.token_in, ...), custom_call_target="tpu_custom_call" | custom-call | tf_op jit(solution)/shard_map/tail/pallas_call | solution.py:759
